TPU v7x, 32 devices: a whole 2x2x4 slice. The times are simulated.
32 devices in a mesh: pair: 16 (over z, x, core), row: 2 (over y).
Axes of the slice: x: 2, y: 2, z: 4, core: 2. Of those that a mesh axis runs over, the one named last changes fastest.
Arguments:
- gram_field: float32 [64, 2, 16, 16, 256], P('pair', None, 'row'), may hold values from -3.6 to 3.6, as said below
- left_variance: float32 [64, 16, 16], P('pair'), may hold values from 0.25 to 4
- right_variance: float32 [2, 16, 16], replicated, may hold values from 0.25 to 4
- cotangent: float32 [64, 2, 8, 8, 64], P('pair', 'row'), may hold values from -24 to 24
Outputs:
- gram_gradient: float32 [64, 2, 16, 16, 256], P('pair', None, 'row')
- left_gradient: float32 [64, 16, 16], P('pair')
- right_gradient: float32 [2, 16, 16], replicated
Inputs may be any that keep to these rules, and one draw needn't show every extreme that they name: `gram_field`: each entry lies within 0.9 times the square root of the product of left_variance and right_variance at its two pixels.
All inputs are finite; a program needn't handle non-finite values.
Results may differ from a plain program's by a relative error of at most 0.00008.
Values sent between devices are 32-bit elements; how exact they have to be, the bound alone decides.
A program may use at most 64 MiB of HBM per device.

v0:
```python
import jax
import jax.numpy as jnp
from jax import lax
from jax.sharding import PartitionSpec as P


def padded_2(block, sides, width):
    for axis, dim in sides:
        count = lax.axis_size(axis)
        forward = [(i, i + 1) for i in range(count - 1)]
        backward = [(target, source) for source, target in forward]
        low = lax.ppermute(
            lax.slice_in_dim(block, block.shape[dim] - width, None, axis=dim), axis, forward
        )
        high = lax.ppermute(lax.slice_in_dim(block, 0, width, axis=dim), axis, backward)
        block = jnp.concatenate([low, block, high], axis=dim)
    return block


def shifted(source, dimension, offset):
    dimension = dimension % source.ndim
    extent = source.shape[dimension]
    margin = abs(offset)
    widths = [(0, 0)] * source.ndim
    widths[dimension] = (margin, margin)
    padded = jnp.pad(source, widths)
    return lax.slice_in_dim(padded, margin + offset, margin + offset + extent, axis=dimension)


def column_masks(length):
    column_index = jnp.arange(length * length) % length
    return (
        (column_index + 1 < length).astype(jnp.float32),
        (column_index >= 1).astype(jnp.float32),
    )


def mix_columns(source, length):
    mask_up, mask_down = column_masks(length)
    return (
        source
        + shifted(shifted(source, -2, 1), -1, 1) * mask_up
        + shifted(shifted(source, -2, -1), -1, -1) * mask_down
    )


def conv_field(padded, length):
    inner = (
        padded[..., 1:-1, :, :]
        + shifted(padded[..., 2:, :, :], -1, length)
        + shifted(padded[..., :-2, :, :], -1, -length)
    )
    return mix_columns(inner, length) / 9.0


def pad_rows(source):
    widths = [(0, 0)] * source.ndim
    widths[source.ndim - 3] = (1, 1)
    return jnp.pad(source, widths)


def conv_map(source):
    row_sum = source + shifted(source, -2, 1) + shifted(source, -2, -1)
    return (row_sum + shifted(row_sum, -1, 1) + shifted(row_sum, -1, -1)) / 9.0


def pool_field(source):
    shape = source.shape
    leading = shape[:-3]
    count = shape[-3]
    length = shape[-2]
    half_side = length // 2
    merged = source.reshape(shape[:-1] + (half_side, 2 * length))
    merged = merged[..., :length] + merged[..., length:]
    merged = merged.reshape(shape[:-1] + (half_side * length,))
    merged = merged[..., 0::2] + merged[..., 1::2]
    merged = merged.reshape(leading + (count // 2, 2, half_side, 2, half_side * half_side))
    return jnp.sum(merged, axis=(-4, -2)) / 16.0


def spread_field(source):
    half_side = source.shape[-2]
    merged = jnp.repeat(source, 2, axis=-3)
    merged = jnp.repeat(merged, 2, axis=-2)
    inner = merged.shape[:-1]
    merged = merged.reshape(inner + (half_side, 1, half_side, 1))
    merged = jnp.broadcast_to(merged, inner + (half_side, 2, half_side, 2))
    return merged.reshape(inner + (4 * half_side * half_side,)) / 16.0


def pool_map(source):
    extent = source.shape[-1] // 2
    merged = source.reshape(source.shape[:-2] + (extent, 2, extent, 2))
    return jnp.mean(merged, axis=(-3, -1))


def spread_map(source):
    return jnp.repeat(jnp.repeat(source, 2, axis=-2), 2, axis=-1) / 4.0


def arc_kernel(source, left, right):
    magnitude = jnp.sqrt(left * right)
    cosine = source / magnitude
    angle_part = jnp.pi - jnp.arccos(cosine)
    sine_part = jnp.sqrt(1.0 - cosine * cosine)
    kernel = magnitude * (sine_part + angle_part * cosine) / (2.0 * jnp.pi)
    slopes = angle_part / (2.0 * jnp.pi)
    weights = magnitude * sine_part / (4.0 * jnp.pi)
    return (kernel, slopes, weights)


def row_window(source, first, count):
    padded = jnp.pad(source, ((0, 0), (2, 2), (0, 0)), constant_values=1.0)
    return lax.dynamic_slice_in_dim(padded, first + 2, count, axis=1)


def on_device(gram_field, left_variance, right_variance, cotangent):
    left_count = gram_field.shape[0]
    shard_rows = gram_field.shape[2]
    length = gram_field.shape[3]
    half_side = length // 2
    count = right_variance.shape[0]
    part_count = cotangent.shape[1]
    rank = lax.axis_index("row")
    zero = rank * 0
    start = rank * shard_rows
    first_left = conv_map(left_variance)
    first_right = conv_map(right_variance)
    right_flat = first_right.reshape(1, count, 1, 1, length * length)
    second_left = conv_map(pool_map(first_left / 2.0))
    second_right = conv_map(pool_map(first_right / 2.0)).reshape(count, half_side * half_side)
    padded = padded_2(gram_field, (("row", 2),), 1)
    source_one = conv_field(padded, length)
    left_rows = row_window(first_left, start, shard_rows)
    kernel_one, slope_one, weight_one = arc_kernel(
        source_one, left_rows[:, None, :, :, None], right_flat
    )
    pooled = pool_field(kernel_one)
    gathered = lax.all_to_all(pooled, "row", split_axis=1, concat_axis=2, tiled=True)
    source_two = conv_field(pad_rows(gathered), half_side)
    first_image = rank * part_count
    second_part = lax.dynamic_slice_in_dim(second_right, first_image, part_count, axis=0)
    unused, slope_two, weight_two = arc_kernel(
        source_two, second_left[:, None, :, :, None], second_part[None, :, None, None, :]
    )
    weighted_two = cotangent * weight_two
    left_two = jnp.sum(weighted_two, axis=(1, 4)) / second_left
    right_part = jnp.sum(weighted_two, axis=(0, 2, 3)) / second_part
    right_two = lax.dynamic_update_slice(
        jnp.zeros((count, half_side * half_side), jnp.float32), right_part, (first_image, zero)
    )
    back_local = conv_field(pad_rows(cotangent * slope_two), half_side)
    back_pooled = lax.all_to_all(back_local, "row", split_axis=2, concat_axis=1, tiled=True)
    back_one = spread_field(back_pooled)
    grad_padded = padded_2(back_one * slope_one, (("row", 2),), 1)
    gram_gradient = conv_field(grad_padded, length)
    weighted_one = back_one * weight_one
    left_local = jnp.sum(weighted_one, axis=(1, 4)) / left_rows
    left_placed = lax.dynamic_update_slice(
        jnp.zeros((left_count, length, length), jnp.float32), left_local, (zero, start, zero)
    )
    left_one = spread_map(conv_map(left_two)) / 2.0 + left_placed
    right_local = jnp.sum(weighted_one, axis=(0, 2, 3)) / first_right.reshape(
        count, length * length
    )
    right_one = spread_map(
        conv_map(right_two.reshape(count, half_side, half_side))
    ) / 2.0 + right_local.reshape(count, length, length)
    left_total = lax.psum(left_one, "row")
    right_total = lax.psum(right_one, ("pair", "row"))
    return (gram_gradient, conv_map(left_total), conv_map(right_total))


def solution(mesh):
    in_specs = (
        P("pair", None, "row", None, None),
        P("pair", None, None),
        P(),
        P("pair", "row", None, None, None),
    )
    out_specs = (P("pair", None, "row", None, None), P("pair", None, None), P())
    return jax.shard_map(
        on_device, mesh=mesh, in_specs=in_specs, out_specs=out_specs, check_vma=False
    )
```

profile of v0, /device:TPU:0, one launch (start us, length us, event | category | flops | bytes accessed | tf_op | source)
XLA Modules:
  0.0 147.3 jit_solution(1810867516955323237)
XLA Ops:
  0.6 1.1 fusion.58
  1.7 1.3 collective-permute-start
  3.0 4.9 %collective-permute-start.1 = (f32[4,2,1,16,256]{4,3,2,1,0:T(8,128)S(1)}, f32[4,2,1,16,256]{4,3,2,1,0:T(8,128)S(1)}, u32[]{:S(2)}, u32[]{:S(2)}) collective-permute-start(f32[4,2,1,16,256]{4,3,2,1,0:T(8,128)S(1)} %get-tuple-element.41), channel_id=1, source_target_pairs={{0,1},{2,3},{4,5},{6,7},{8,9},{10,11},{12,13},{14,15},{16,17},{18,... | collective-permute-start | bytes 393224 | tf_op jit(solution)/shard_map/ppermute | solution.py:12
  12.3 3.2 %multiply_multiply_fusion.2 = (f32[4,2,8,16,256]{4,3,2,1,0:T(8,128)S(1)}, f32[4,2,8,16,256]{4,3,2,1,0:T(8,128)S(1)}) fusion(f32[2,256]{1,0:T(2,128)S(1)} %mul.137, f32[4,8,16]{2,1,0:T(8,128)S(1)} %pad_dynamic-slice_fusion, f32[256]{0:T(256)S(1)} %get-tuple-element.54, f32[4,2,8,16,256]{4,3,2,1,0:T(8,128)S(1)} %get-tuple-element.39, ...), kind=kLoop, calls=%fused_computation.44 | loop fusion | flops 8650752 | bytes 5511168 | tf_op jit(solution)/shard_map/div | solution.py:106
  15.5 2.4 %reshape.113 = f32[4,2,8,16,8,32]{5,4,3,2,1,0:T(8,128)} reshape(f32[4,2,8,16,256]{4,3,2,1,0:T(8,128)S(1)} %get-tuple-element.31) | data formatting | bytes 2097152 | tf_op jit(solution)/shard_map/reshape | solution.py:73
  17.9 6.6 %slice_add_fusion = f32[4,2,8,16,8,16]{5,4,3,2,1,0:T(8,128)} fusion(f32[4,2,8,16,8,32]{5,4,3,2,1,0:T(8,128)} %reshape.113), kind=kLoop, calls=%fused_computation | loop fusion | flops 131072 | bytes 1572864 | tf_op jit(solution)/shard_map/add | solution.py:74
  24.5 3.2 %reshape.114 = f32[4,2,8,16,128]{4,3,2,1,0:T(8,128)S(1)} reshape(f32[4,2,8,16,8,16]{5,4,3,2,1,0:T(8,128)} %slice_add_fusion) | data formatting | bytes 1048576 | tf_op jit(solution)/shard_map/reshape | solution.py:75
  27.8 9.4 %slice.243 = f32[4,2,8,16,64]{4,3,2,1,0:T(8,128)S(1)} slice(f32[4,2,8,16,128]{4,3,2,1,0:T(8,128)S(1)} %reshape.114), slice={[0:4:1], [0:2:1], [0:8:1], [0:16:1], [1:128:2]} | slice | bytes 524288 | tf_op jit(solution)/shard_map/slice | solution.py:76
  37.1 9.2 %slice.242 = f32[4,2,8,16,64]{4,3,2,1,0:T(8,128)S(1)} slice(f32[4,2,8,16,128]{4,3,2,1,0:T(8,128)S(1)} %reshape.114), slice={[0:4:1], [0:2:1], [0:8:1], [0:16:1], [0:128:2]} | slice | bytes 524288 | tf_op jit(solution)/shard_map/slice | solution.py:76
  47.7 3.3 %all-to-all-start = ((f32[2,1,8192]{2,1,0:T(1,128)}), f32[2,1,8192]{2,1,0:T(1,128)S(1)}, u32[]{:S(2)}, u32[]{:S(2)}) async-start(f32[2,1,8192]{2,1,0:T(1,128)} %reshape.120), calls=%async_computation | async-start | bytes 131072 | tf_op jit(solution)/shard_map/all_to_all | solution.py:139
  51.1 4.0 %all-to-all-done = f32[2,1,8192]{2,1,0:T(1,128)S(1)} async-done(((f32[2,1,8192]{2,1,0:T(1,128)}), f32[2,1,8192]{2,1,0:T(1,128)S(1)}, u32[]{:S(2)}, u32[]{:S(2)}) %all-to-all-start) | async-done | bytes 65568 | tf_op jit(solution)/shard_map/all_to_all | solution.py:139
  59.0 3.5 %all-to-all-start.1 = ((f32[2,1,8192]{2,1,0:T(1,128)}), f32[2,1,8192]{2,1,0:T(1,128)S(1)}, u32[]{:S(2)}, u32[]{:S(2)}) async-start(f32[2,1,8192]{2,1,0:T(1,128)} %reshape.122), calls=%async_computation.1 | async-start | bytes 131072 | tf_op jit(solution)/shard_map/all_to_all | solution.py:153
  63.0 3.5 %all-to-all-done.1 = f32[2,1,8192]{2,1,0:T(1,128)S(1)} async-done(((f32[2,1,8192]{2,1,0:T(1,128)}), f32[2,1,8192]{2,1,0:T(1,128)S(1)}, u32[]{:S(2)}, u32[]{:S(2)}) %all-to-all-start.1) | async-done | bytes 65568 | tf_op jit(solution)/shard_map/all_to_all | solution.py:153
  67.7 2.5 %div.167 = f32[4,2,8,16,8,8]{5,4,2,3,1,0:T(8,128)} reshape(f32[4,2,8,8,2,64]{5,2,4,3,1,0:T(8,128)S(1)} %broadcast_in_dim.17) | data formatting | bytes 524288 | tf_op jit(solution)/shard_map/div | solution.py:88
  70.2 3.6 %copy.184 = f32[4,2,8,16,8,8]{3,2,5,4,1,0:T(8,128)S(1)} copy(f32[4,2,8,16,8,8]{5,4,2,3,1,0:T(8,128)} %div.167) | data formatting | bytes 524288 | tf_op jit(solution)/shard_map/div | solution.py:88
  73.9 4.0 %broadcast_in_dim.18 = f32[4,2,8,16,8,2,8,2]{3,2,7,6,5,4,1,0:T(8,128)} broadcast(f32[4,2,8,16,8,8]{3,2,5,4,1,0:T(8,128)S(1)} %copy.184), dimensions={0,1,2,3,4,6} | broadcast | bytes 1310720 | tf_op jit(solution)/shard_map/broadcast_in_dim | solution.py:87
  77.8 5.1 %copy.185 = f32[4,2,8,16,256]{4,3,2,1,0:T(8,128)S(1)} copy(f32[4,2,8,16,256]{3,2,4,1,0:T(8,128)} %bitcast.36) | data formatting | bytes 2097152 | tf_op jit(solution)/shard_map/div | solution.py:88
  83.0 2.8 %fusion.40 = (f32[2,256]{1,0:T(2,128)S(1)}, f32[4,8,16]{2,1,0:T(8,128)S(1)}, f32[4,2,8,16,256]{4,3,2,1,0:T(8,128)S(1)}) fusion(f32[4,2,8,16,256]{4,3,2,1,0:T(8,128)S(1)} %copy.185, f32[4,2,8,16,256]{4,3,2,1,0:T(8,128)S(1)} %get-tuple-element.32, f32[2,256]{1,0:T(2,128)S(1)} %mul.137, f32[4,8,16]{2,1,0:T(8,128)S(1)} %pad_dynamic-slice_fusion), kind=kLoop, calls=%fused_computation.104 | loop fusion | flops 3668992 | bytes 3153920 | tf_op jit(solution)/shard_map/reduce_sum | solution.py:163
  85.8 7.0 %psum.14 = f32[4,16,16]{2,1,0:T(8,128)S(1)} all-reduce(f32[4,16,16]{2,1,0:T(8,128)S(1)} %add_dynamic-update-slice_fusion), channel_id=1, replica_groups=mesh['pair'=16,'row'=2] {'row'}, use_global_device_ids=true, to_apply=%region_5.6 | all-reduce | flops 1024 | bytes 8192 | tf_op jit(solution)/shard_map/psum | solution.py:169
  93.0 42.1 %psum.15 = f32[2,16,16]{1,2,0:T(8,128)S(1)} all-reduce(f32[2,16,16]{1,2,0:T(8,128)S(1)} %divide_add_fusion), channel_id=1, replica_groups=mesh['pair'=16,'row'=2] {'pair','row'}, use_global_device_ids=true, to_apply=%region_8.9 | all-reduce | flops 512 | bytes 4096 | tf_op jit(solution)/shard_map/psum | solution.py:170
  135.9 1.3 collective-permute-start.2
  137.2 4.6 %collective-permute-start.3 = (f32[4,2,1,16,256]{4,3,2,1,0:T(8,128)S(1)}, f32[4,2,1,16,256]{4,3,2,1,0:T(8,128)S(1)}, u32[]{:S(2)}, u32[]{:S(2)}) collective-permute-start(f32[4,2,1,16,256]{4,3,2,1,0:T(8,128)S(1)} %get-tuple-element.37), channel_id=1, source_target_pairs={{0,1},{2,3},{4,5},{6,7},{8,9},{10,11},{12,13},{14,15},{16,17},{18,... | collective-permute-start | bytes 393224 | tf_op jit(solution)/shard_map/ppermute | solution.py:12
  142.8 1.5 %collective-permute-done.3 = f32[4,2,1,16,256]{4,3,2,1,0:T(8,128)S(1)} collective-permute-done((f32[4,2,1,16,256]{4,3,2,1,0:T(8,128)S(1)}, f32[4,2,1,16,256]{4,3,2,1,0:T(8,128)S(1)}, u32[]{:S(2)}, u32[]{:S(2)}) %collective-permute-start.3) | collective-permute-done | bytes 131104 | tf_op jit(solution)/shard_map/ppermute | solution.py:12
  145.2 2.1 %fusion.9 = f32[4,2,8,16,256]{4,3,2,1,0:T(8,128)} fusion(f32[4,2,8,16,256]{4,3,2,1,0:T(8,128)S(1)} %get-tuple-element.35, f32[4,2,8,16,256]{4,3,2,1,0:T(8,128)S(1)} %get-tuple-element.34, f32[256]{0:T(256)S(1)} %get-tuple-element.54, f32[256]{0:T(256)S(1)} %get-tuple-element.55, f32[4,2,8,16,256]{4,3,2,1,0:T(8,128)S(1)} %get-tuple-element.33, ...), kind=kLoop, calls=%fused_computation.18 | loop fusion | flops 5505024 | bytes 4458496 | tf_op jit(solution)/shard_map/div | solution.py:53
  (92 shorter events, 14.0 us)
Async XLA Ops:
  0.6 10.7 %copy-start = (f32[4,2,8,16,256]{4,3,2,1,0:T(8,128)S(1)}, f32[4,2,8,16,256]{4,3,2,1,0:T(8,128)}, u32[]{:S(2)}) copy-start(f32[4,2,8,16,256]{4,3,2,1,0:T(8,128)} %param.4) | copy-start | bytes 3145732
  1.7 9.6 %collective-permute-start = (f32[4,2,1,16,256]{4,3,2,1,0:T(8,128)S(1)}, f32[4,2,1,16,256]{4,3,2,1,0:T(8,128)S(1)}, u32[]{:S(2)}, u32[]{:S(2)}) collective-permute-start(f32[4,2,1,16,256]{4,3,2,1,0:T(8,128)S(1)} %get-tuple-element.40), channel_id=1, source_target_pairs={{1,0},{3,2},{5,4},{7,6},{9,8},{11,10},{13,12},{15,14},{17,16},{19,... | collective-permute-start | bytes 393224 | tf_op jit(solution)/shard_map/ppermute | solution.py:15
  3.0 8.3 %collective-permute-start.1 = (f32[4,2,1,16,256]{4,3,2,1,0:T(8,128)S(1)}, f32[4,2,1,16,256]{4,3,2,1,0:T(8,128)S(1)}, u32[]{:S(2)}, u32[]{:S(2)}) collective-permute-start(f32[4,2,1,16,256]{4,3,2,1,0:T(8,128)S(1)} %get-tuple-element.41), channel_id=1, source_target_pairs={{0,1},{2,3},{4,5},{6,7},{8,9},{10,11},{12,13},{14,15},{16,17},{18,... | collective-permute-start | bytes 393224 | tf_op jit(solution)/shard_map/ppermute | solution.py:12
  46.4 10.6 %copy-start.1 = (f32[4,1,8,8,64]{4,3,2,1,0:T(8,128)S(1)}, f32[4,1,8,8,64]{4,3,2,1,0:T(8,128)}, u32[]{:S(2)}) copy-start(f32[4,1,8,8,64]{4,3,2,1,0:T(8,128)} %param.7) | copy-start | bytes 196612
  46.4 10.6 %copy-start.2 = (f32[64]{0:T(128)S(1)}, f32[64]{0:T(128)}, u32[]{:S(2)}) copy-start(f32[64]{0:T(128)} %get-tuple-element.52) | copy-start | bytes 772
  46.4 10.6 %copy-start.3 = (f32[64]{0:T(128)S(1)}, f32[64]{0:T(128)}, u32[]{:S(2)}) copy-start(f32[64]{0:T(128)} %get-tuple-element.53) | copy-start | bytes 772
  47.7 7.4 %all-to-all-start = ((f32[2,1,8192]{2,1,0:T(1,128)}), f32[2,1,8192]{2,1,0:T(1,128)S(1)}, u32[]{:S(2)}, u32[]{:S(2)}) async-start(f32[2,1,8192]{2,1,0:T(1,128)} %reshape.120), calls=%async_computation | async-start | bytes 131072 | tf_op jit(solution)/shard_map/all_to_all | solution.py:139
  59.0 7.4 %all-to-all-start.1 = ((f32[2,1,8192]{2,1,0:T(1,128)}), f32[2,1,8192]{2,1,0:T(1,128)S(1)}, u32[]{:S(2)}, u32[]{:S(2)}) async-start(f32[2,1,8192]{2,1,0:T(1,128)} %reshape.122), calls=%async_computation.1 | async-start | bytes 131072 | tf_op jit(solution)/shard_map/all_to_all | solution.py:153
  135.9 6.9 %collective-permute-start.2 = (f32[4,2,1,16,256]{4,3,2,1,0:T(8,128)S(1)}, f32[4,2,1,16,256]{4,3,2,1,0:T(8,128)S(1)}, u32[]{:S(2)}, u32[]{:S(2)}) collective-permute-start(f32[4,2,1,16,256]{4,3,2,1,0:T(8,128)S(1)} %get-tuple-element.36), channel_id=1, source_target_pairs={{1,0},{3,2},{5,4},{7,6},{9,8},{11,10},{13,12},{15,14},{17,16},{19,... | collective-permute-start | bytes 393224 | tf_op jit(solution)/shard_map/ppermute | solution.py:15
  137.2 7.1 %collective-permute-start.3 = (f32[4,2,1,16,256]{4,3,2,1,0:T(8,128)S(1)}, f32[4,2,1,16,256]{4,3,2,1,0:T(8,128)S(1)}, u32[]{:S(2)}, u32[]{:S(2)}) collective-permute-start(f32[4,2,1,16,256]{4,3,2,1,0:T(8,128)S(1)} %get-tuple-element.37), channel_id=1, source_target_pairs={{0,1},{2,3},{4,5},{6,7},{8,9},{10,11},{12,13},{14,15},{16,17},{18,... | collective-permute-start | bytes 393224 | tf_op jit(solution)/shard_map/ppermute | solution.py:12
where the time goes:
time: 148 us; the launch traced here: 147 us
  blocking collectives  49.2 us (33%)
  local copies, waits for them, and re-layouts  46.9 us (32%)
  other arithmetic  22.1 us (15%)
  starting transfers between devices  18.8 us (13%)
  waiting for transfers between devices  9.22 us (6%)
    psum x1, blocking collectives, on_device(): right_total = lax.psum(right_one, ('pair', 'row'))  42.1 us
    slice x2, local copies, waits for them, and re-layouts, pool_field(): merged = merged[..., 0::2] + merged[..., 1::2]  18.6 us
    div x4, local copies, waits for them, and re-layouts, spread_field(): return merged.reshape(inner + (4 * half_side * half_side,)) / 16.0  11.4 us
    ppermute x2, starting transfers between devices, padded_2(): lax.ppermute(lax.slice_in_dim(block, block.shape[dim] - width, None, axis...  9.44 us
    psum x1, blocking collectives, on_device(): left_total = lax.psum(left_one, 'row')  7.05 us
    add x1, other arithmetic, pool_field(): merged = merged[..., :length] + merged[..., length:]  6.58 us
    all_to_all x1, waiting for transfers between devices, on_device(): lax.all_to_all(pooled, 'row', split_axis=1, concat_axis=2, tiled=True)  3.97 us
    broadcast_in_dim x1, local copies, waits for them, and re-layouts, spread_field(): merged = jnp.broadcast_to(merged, inner + (half_side, 2, half_side, 2))  3.95 us
  transfers between devices with their start and end apart: 6, of which 4 were waited for; matrix products, arithmetic and copies ran while one was open for 3% of the time, Pallas kernels for 0%

commit v1 on v0

v1 whole, which is shorter than its diff:
```python
import functools
import math

import jax
import jax.numpy as jnp
import numpy as np
from jax import lax
from jax.experimental import pallas as pl
from jax.experimental.pallas import tpu as pltpu
from jax.sharding import PartitionSpec as P

ARCSIN_EVEN = (2.61397078, -1.36807576, 0.342139678, -0.0179491288)
ARCSIN_ROOT = (-1.61397053, 0.727749535, -0.104947558)


def conv_map(source):
    padded = jnp.pad(source, ((0, 0), (1, 1), (1, 1)))
    n = source.shape[-1]
    rows = padded[:, 0:n] + padded[:, 1 : n + 1] + padded[:, 2 : n + 2]
    return (rows[:, :, 0:n] + rows[:, :, 1 : n + 1] + rows[:, :, 2 : n + 2]) / 9.0


def pool_map(source):
    extent = source.shape[-1] // 2
    merged = source.reshape(source.shape[:-2] + (extent, 2, extent, 2))
    return jnp.mean(merged, axis=(-3, -1))


def spread_map(source):
    return jnp.repeat(jnp.repeat(source, 2, axis=-2), 2, axis=-1) / 4.0


def pool_matrices(length, group):
    half = length // 2
    width = half * half
    matrix = np.zeros((group, length * length, group * width), np.float32)
    for k in range(length):
        for l in range(length):
            for b in range(group):
                matrix[b, k * length + l, b * width + (k // 2) * half + l // 2] = 1.0
    return jnp.asarray(matrix, jnp.bfloat16)


def split_dot(x, matrix, dims):
    high = x.astype(jnp.bfloat16)
    low = (x - high.astype(jnp.float32)).astype(jnp.bfloat16)
    dot = functools.partial(
        lax.dot_general, dimension_numbers=(dims, ((), ())), preferred_element_type=jnp.float32
    )
    return dot(high, matrix) + dot(low, matrix)


def arc_parts(rho):
    square = rho * rho
    rest = 1.0 - square
    sine = rest * lax.rsqrt(rest)
    even = ARCSIN_EVEN[3]
    for c in ARCSIN_EVEN[2::-1]:
        even = even * square + c
    root = ARCSIN_ROOT[2]
    for c in ARCSIN_ROOT[1::-1]:
        root = root * square + c
    angle = (0.5 * math.pi) + rho * (even + sine * root)
    return sine, angle


def lane_masks(shape, side):
    lane = lax.broadcasted_iota(jnp.int32, shape, 1)
    sub = lax.broadcasted_iota(jnp.int32, shape, 0)
    col = lax.rem(lane, side)
    k = lax.rem(lane // side, side)
    k_up = k + 1 < side
    k_down = k >= 1
    v_up = (col + 1 < side) & (sub + 1 < shape[0])
    v_down = (col >= 1) & (sub >= 1)
    return k_up, k_down, v_up, v_down


def roll(x, shift, axis):
    return pltpu.roll(x, shift % x.shape[axis], axis)


def conv_rows(rows, side, masks):
    k_up, k_down, v_up, v_down = masks
    out = []
    for i in range(1, len(rows) - 1):
        inner = rows[i]
        if rows[i + 1] is not None:
            inner = inner + jnp.where(k_up, roll(rows[i + 1], -side, 1), 0.0)
        if rows[i - 1] is not None:
            inner = inner + jnp.where(k_down, roll(rows[i - 1], side, 1), 0.0)
        up = jnp.where(v_up, roll(roll(inner, -1, 0), -1, 1), 0.0)
        down = jnp.where(v_down, roll(roll(inner, 1, 0), 1, 1), 0.0)
        out.append(inner + up + down)
    return out


def body(
    sizes,
    gram_hbm, cot_hbm, gl_ref, il_ref, gr_ref, ir_ref, gl2_ref, il2_ref, gr2_ref, ir2_ref, mat_ref,
    out_hbm, left_out, right_out, left2_out,
    gram, cot, slope, sinem, kp, tmp, pooled, back, fine, wsum, wsum2, racc, out_v, left_all, pair_all, packet,
    load_sem, out_sem, halo_send, halo_recv, cot_send, cot_recv, pool_send, pool_recv,
    slope_send, slope_recv, left_send, left_recv, pair_send, pair_recv,
):
    n, npair, A, B, rows, R, group, part = sizes
    H = R // 2
    W = R * R
    G = B // group
    PR = rows // 2
    width = H * H
    me = lax.axis_index("row")
    mine = lax.axis_index("pair")

    loads = []
    for a in range(A):
        c = pltpu.make_async_copy(gram_hbm.at[a], gram.at[a, :, pl.ds(1, rows)], load_sem.at[a])
        c.start()
        loads.append(c)
    cot_load = pltpu.make_async_copy(cot_hbm, cot.at[me], load_sem.at[A])
    cot_load.start()

    barrier = pltpu.get_barrier_semaphore()
    for d in range(1, n):
        pl.semaphore_signal(barrier, inc=1, device_id={"row": lax.rem(me + d, n)})
    for d in range(1, npair):
        pl.semaphore_signal(barrier, inc=1, device_id={"pair": lax.rem(mine + d, npair)})
    pl.semaphore_wait(barrier, n - 1 + npair - 1)

    has_low = me > 0
    has_high = me < n - 1
    low = jnp.maximum(me - 1, 0)
    high = jnp.minimum(me + 1, n - 1)

    def halo_up():
        return pltpu.make_async_remote_copy(
            src_ref=gram_hbm.at[:, :, rows - 1], dst_ref=gram.at[:, :, 0],
            send_sem=halo_send.at[0], recv_sem=halo_recv.at[0], device_id={"row": high})

    def halo_down():
        return pltpu.make_async_remote_copy(
            src_ref=gram_hbm.at[:, :, 0], dst_ref=gram.at[:, :, rows + 1],
            send_sem=halo_send.at[1], recv_sem=halo_recv.at[1], device_id={"row": low})

    def slope_up():
        return pltpu.make_async_remote_copy(
            src_ref=slope.at[:, :, rows], dst_ref=slope.at[:, :, 0],
            send_sem=slope_send.at[0], recv_sem=slope_recv.at[0], device_id={"row": high})

    def slope_down():
        return pltpu.make_async_remote_copy(
            src_ref=slope.at[:, :, 1], dst_ref=slope.at[:, :, rows + 1],
            send_sem=slope_send.at[1], recv_sem=slope_recv.at[1], device_id={"row": low})

    def row_copy(ref, sends, recvs, d):
        return pltpu.make_async_remote_copy(
            src_ref=ref.at[me], dst_ref=ref.at[me], send_sem=sends.at[d],
            recv_sem=recvs.at[me], device_id={"row": lax.rem(me + d, n)})

    def row_arrival(ref, sends, recvs, d):
        source = lax.rem(me + d, n)
        return pltpu.make_async_remote_copy(
            src_ref=ref.at[source], dst_ref=ref.at[source], send_sem=sends.at[d],
            recv_sem=recvs.at[source], device_id={"row": source})

    @pl.when(has_high)
    def _():
        halo_up().start()

    @pl.when(has_low)
    def _():
        halo_down().start()

    zero_row = jnp.zeros((A, B, R, W), jnp.float32)

    @pl.when(jnp.logical_not(has_low))
    def _():
        gram[:, :, 0] = zero_row
        slope[:, :, 0] = zero_row

    @pl.when(jnp.logical_not(has_high))
    def _():
        gram[:, :, rows + 1] = zero_row
        slope[:, :, rows + 1] = zero_row

    cot_load.wait()
    for d in range(1, n):
        row_copy(cot, cot_send, cot_recv, d).start()
    for c in loads:
        c.wait()

    masks = lane_masks((R, W), R)

    def forward(a, b, p):
        f = [gram[a, b, 2 * p + t] for t in range(4)]
        source = conv_rows(f, R, masks)
        total = None
        for t in range(2):
            i = 2 * p + t
            gl = gl_ref[a, i]
            il = il_ref[a, i]
            gl = jnp.concatenate([gl] * (W // 128), axis=1)
            il = jnp.concatenate([il] * (W // 128), axis=1)
            m = gl * gr_ref[b][None, :]
            rho = source[t] * (il * ir_ref[b][None, :])
            sine, angle = arc_parts(rho)
            sm = m * sine
            slope[a, b, i + 1] = angle
            sinem[a, b, i] = sm
            term = sm + m * (angle * rho)
            total = term if total is None else total + term
        kp[a, b, p] = total

    interior = list(range(1, PR - 1))
    edges = sorted({0, PR - 1})

    if interior:
        @pl.loop(0, A)
        def _(a):
            for b in range(B):
                for p in interior:
                    forward(a, b, p)

    @pl.when(has_low)
    def _():
        halo_up().wait_recv()

    @pl.when(has_high)
    def _():
        halo_down().wait_recv()

    @pl.loop(0, A)
    def _(a):
        for b in range(B):
            for p in edges:
                forward(a, b, p)
        for g in range(G):
            acc = None
            for t in range(group):
                x = kp[a, g * group + t].reshape(PR * R, W)
                y = split_dot(x, mat_ref[t], ((1,), (0,)))
                acc = y if acc is None else acc + y
            tmp[g] = acc
            even = tmp[g, pl.ds(0, PR * H, stride=2), :]
            odd = tmp[g, pl.ds(1, PR * H, stride=2), :]
            pooled[me, a, g] = ((even + odd) * (1.0 / (32.0 * math.pi))).reshape(PR, H, 128)

    for d in range(1, n):
        row_copy(pooled, pool_send, pool_recv, d).start()

    @pl.when(has_high)
    def _():
        slope_up().start()

    @pl.when(has_low)
    def _():
        slope_down().start()

    for d in range(1, n):
        row_arrival(cot, cot_send, cot_recv, d).wait_recv()
    for d in range(1, n):
        row_arrival(pooled, pool_send, pool_recv, d).wait_recv()

    masks2 = lane_masks((H, 128), H)
    for g in range(G):
        racc[2 * B + g] = jnp.zeros((R, 128), jnp.float32)

    @pl.loop(0, A)
    def _(a):
        left2 = [None] * H
        for g in range(G):
            f = [None] + [pooled[i // PR, a, g, i % PR] for i in range(H)] + [None]
            source = conv_rows(f, H, masks2)
            ct = [None]
            right2 = None
            for i in range(H):
                m = gl2_ref[a, i] * gr2_ref[g][None, :]
                rho = source[i] * (il2_ref[a, i] * ir2_ref[g][None, :])
                sine, angle = arc_parts(rho)
                pieces = []
                for t in range(group):
                    b = g * group + t
                    pieces.append(cot[b // part, a, b % part, i])
                c = jnp.concatenate(pieces, axis=1)
                ct.append(c * angle)
                w = c * (m * sine)
                right2 = w if right2 is None else right2 + w
                left2[i] = w if left2[i] is None else left2[i] + w
            ct.append(None)
            racc[2 * B + g, 0:H] = racc[2 * B + g, 0:H] + right2
            b_rows = conv_rows(ct, H, masks2)
            scale = 1.0 / (9.0 * 2.0 * math.pi * 16.0) / (18.0 * math.pi)
            zero = jnp.zeros((H, 128), jnp.float32)
            back[g, 0] = zero
            back[g, H + 1] = zero
            for i in range(H):
                back[g, i + 1] = b_rows[i] * scale
            x = back[g, pl.ds(me * PR, PR + 2)].reshape((PR + 2) * H, 128)
            for t in range(group):
                y = split_dot(x, mat_ref[t], ((1,), (1,)))
                for h in range(W // 128):
                    part_y = y[:, h * 128 : (h + 1) * 128]
                    fine[a, g * group + t, h, pl.ds(0, (PR + 2) * H, stride=2), :] = part_y
                    fine[a, g * group + t, h, pl.ds(1, (PR + 2) * H, stride=2), :] = part_y
        for i in range(H):
            wsum2[a, i] = left2[i]

    def back_row(a, b, c):
        return jnp.concatenate([fine[a, b, h, c * R : (c + 1) * R, :] for h in range(W // 128)], axis=1)

    racc[0 : 2 * B] = jnp.zeros((2 * B, R, 128), jnp.float32)

    @pl.loop(0, A)
    def _(a):
        lsum = [None] * rows
        for b in range(B):
            total = None
            for p in range(PR):
                bk = back_row(a, b, p + 1)
                for t in range(2):
                    i = 2 * p + t
                    w = bk * sinem[a, b, i]
                    total = w if total is None else total + w
                    lsum[i] = w if lsum[i] is None else lsum[i] + w
            for h in range(W // 128):
                racc[2 * b + h] = racc[2 * b + h] + total[:, h * 128 : (h + 1) * 128]
        for i in range(rows):
            wsum[a, i] = lsum[i]

    ones_bf = jnp.ones((8, W), jnp.bfloat16)

    def lane_sums(x):
        high_part = x.astype(jnp.bfloat16)
        low_part = (x - high_part.astype(jnp.float32)).astype(jnp.bfloat16)
        dims = (((1,), (1,)), ((), ()))
        ones = ones_bf[:, : x.shape[1]]
        return lax.dot_general(ones, high_part, dims, preferred_element_type=jnp.float32) + lax.dot_general(
            ones, low_part, dims, preferred_element_type=jnp.float32)

    nl = A * rows * R // 128
    ls = lane_sums(wsum[...].reshape(A * rows * R, W))
    for c in range(nl):
        left_all[me, 2 * B + G + c : 2 * B + G + c + 1, :] = ls[0:1, c * 128 : (c + 1) * 128]
    left_all[me, 0 : 2 * B + G, :] = jnp.sum(racc[...], axis=1)
    for d in range(1, n):
        row_copy(left_all, left_send, left_recv, d).start()

    ls2 = lane_sums(wsum2[...].reshape(A * H * H, 128))
    for c in range(A * H * H // 128):
        left2_out[c : c + 1, :] = ls2[0:1, c * 128 : (c + 1) * 128]

    def final(a, b, chosen):
        cache = {}

        def product(i):
            if i not in cache:
                cache[i] = back_row(a, b, (i + 1) // 2) * slope[a, b, i]
            return cache[i]

        for i in chosen:
            (value,) = conv_rows([product(i - 1), product(i), product(i + 1)], R, masks)
            out_v[a, b, i - 1] = value

    if rows > 2:
        @pl.loop(0, A)
        def _(a):
            for b in range(B):
                final(a, b, range(2, rows))

    for d in range(1, n):
        row_arrival(left_all, left_send, left_recv, d).wait_recv()
    left_out[...] = left_all[...]
    right = left_all[0, 0 : 2 * B, :]
    for r in range(1, n):
        right = right + left_all[r, 0 : 2 * B, :]
    packet_rows = packet.shape[0]
    packet[...] = jnp.zeros((packet_rows, 128), jnp.float32)
    packet[0 : 2 * B, :] = right
    packet[2 * B : 2 * B + G, :] = left_all[me, 2 * B : 2 * B + G, :]
    pair_all[mine] = packet[...]

    def pair_copy(d):
        return pltpu.make_async_remote_copy(
            src_ref=packet, dst_ref=pair_all.at[mine], send_sem=pair_send.at[d],
            recv_sem=pair_recv.at[mine], device_id={"pair": lax.rem(mine + d, npair)})

    def pair_arrival(d):
        source = lax.rem(mine + d, npair)
        return pltpu.make_async_remote_copy(
            src_ref=packet, dst_ref=pair_all.at[source], send_sem=pair_send.at[d],
            recv_sem=pair_recv.at[source], device_id={"pair": source})

    for d in range(1, npair):
        pair_copy(d).start()

    @pl.when(has_low)
    def _():
        slope_up().wait_recv()

    @pl.when(has_high)
    def _():
        slope_down().wait_recv()

    @pl.loop(0, A)
    def _(a):
        for b in range(B):
            final(a, b, sorted({1, rows}))
        pltpu.make_async_copy(out_v.at[a], out_hbm.at[a], out_sem.at[a]).start()

    for d in range(1, npair):
        pair_arrival(d).wait_recv()
    total = pair_all[0]
    for r in range(1, npair):
        total = total + pair_all[r]
    right_out[...] = total

    for a in range(A):
        pltpu.make_async_copy(out_v.at[a], out_hbm.at[a], out_sem.at[a]).wait()

    @pl.when(has_high)
    def _():
        halo_up().wait_send()
        slope_up().wait_send()

    @pl.when(has_low)
    def _():
        halo_down().wait_send()
        slope_down().wait_send()

    for d in range(1, n):
        row_copy(cot, cot_send, cot_recv, d).wait_send()
        row_copy(pooled, pool_send, pool_recv, d).wait_send()
        row_copy(left_all, left_send, left_recv, d).wait_send()
    for d in range(1, npair):
        pair_copy(d).wait_send()


def on_device(n, npair, gram_field, left_variance, right_variance, cotangent):
    A, B, rows, R, W = gram_field.shape
    part = cotangent.shape[1]
    H = R // 2
    width = H * H
    group = 128 // width
    G = B // group
    PR = rows // 2
    rank = lax.axis_index("row")
    start = rank * rows
    f32 = jnp.float32

    first_left = conv_map(left_variance)
    first_right = conv_map(right_variance)
    second_left = conv_map(pool_map(first_left / 2.0))
    second_right = conv_map(pool_map(first_right / 2.0))
    my_left = lax.dynamic_slice_in_dim(first_left, start, rows, axis=1)
    gl = jnp.broadcast_to(jnp.sqrt(my_left)[..., None], (A, rows, R, 128))
    il = jnp.broadcast_to((lax.rsqrt(my_left) / 9.0)[..., None], (A, rows, R, 128))
    gl2 = jnp.broadcast_to(jnp.sqrt(second_left)[..., None], (A, H, H, 128))
    il2 = jnp.broadcast_to((lax.rsqrt(second_left) / 9.0)[..., None], (A, H, H, 128))
    gr = jnp.sqrt(first_right).reshape(B, W)
    ir = lax.rsqrt(first_right).reshape(B, W)
    gr2 = jnp.sqrt(second_right).reshape(G, 128)
    ir2 = lax.rsqrt(second_right).reshape(G, 128)
    mats = pool_matrices(R, group)

    nl = A * rows * R // 128
    left_rows = -(-(2 * B + G + nl) // 8) * 8
    pair_rows = -(-(2 * B + G) // 8) * 8
    sizes = (n, npair, A, B, rows, R, group, part)
    vmem = pl.BlockSpec(memory_space=pltpu.VMEM)
    hbm = pl.BlockSpec(memory_space=pl.ANY)
    dma = pltpu.SemaphoreType.DMA
    out, left, right, left2 = pl.pallas_call(
        functools.partial(body, sizes),
        out_shape=(
            jax.ShapeDtypeStruct(gram_field.shape, f32),
            jax.ShapeDtypeStruct((n, left_rows, 128), f32),
            jax.ShapeDtypeStruct((pair_rows, 128), f32),
            jax.ShapeDtypeStruct((A * H * H // 128, 128), f32),
        ),
        in_specs=[hbm, hbm] + [vmem] * 9,
        out_specs=(hbm, vmem, vmem, vmem),
        scratch_shapes=[
            pltpu.VMEM((A, B, rows + 2, R, W), f32),
            pltpu.VMEM((n, A, part, H, H, width), f32),
            pltpu.VMEM((A, B, rows + 2, R, W), f32),
            pltpu.VMEM((A, B, rows, R, W), f32),
            pltpu.VMEM((A, B, PR, R, W), f32),
            pltpu.VMEM((G, PR * R, 128), f32),
            pltpu.VMEM((n, A, G, PR, H, 128), f32),
            pltpu.VMEM((G, H + 2, H, 128), f32),
            pltpu.VMEM((A, B, W // 128, (PR + 2) * R, 128), f32),
            pltpu.VMEM((A, rows, R, W), f32),
            pltpu.VMEM((A, H, H, 128), f32),
            pltpu.VMEM((2 * B + G, R, 128), f32),
            pltpu.VMEM((A, B, rows, R, W), f32),
            pltpu.VMEM((n, left_rows, 128), f32),
            pltpu.VMEM((npair, pair_rows, 128), f32),
            pltpu.VMEM((pair_rows, 128), f32),
            dma((A + 1,)), dma((A,)), dma((2,)), dma((2,)),
            dma((n,)), dma((n,)), dma((n,)), dma((n,)),
            dma((2,)), dma((2,)), dma((n,)), dma((n,)), dma((npair,)), dma((npair,)),
        ],
        compiler_params=pltpu.CompilerParams(
            collective_id=0, has_side_effects=True, vmem_limit_bytes=48 * 1024 * 1024
        ),
        name="arc_reverse",
    )(gram_field, cotangent, gl, il, gr, ir, gl2, il2, gr2, ir2, mats)

    left_sum = left[:, 2 * B + G : 2 * B + G + nl].reshape(n, A, rows, R)
    left_sum = left_sum.transpose(1, 0, 2, 3).reshape(A, n * rows, R) * 4.5
    left_two = left2.reshape(A, H, H) / (4.0 * math.pi) / second_left
    left_one = spread_map(conv_map(left_two)) / 2.0 + left_sum / first_left
    right_sum = right[: 2 * B].reshape(B, R, R) * 4.5
    right_two = right[2 * B : 2 * B + G].reshape(B, H, H) / (4.0 * math.pi) / second_right
    right_one = spread_map(conv_map(right_two)) / 2.0 + right_sum / first_right
    return out, conv_map(left_one), conv_map(right_one)


def solution(mesh):
    in_specs = (
        P("pair", None, "row", None, None),
        P("pair", None, None),
        P(),
        P("pair", "row", None, None, None),
    )
    out_specs = (P("pair", None, "row", None, None), P("pair", None, None), P())
    return jax.shard_map(
        functools.partial(on_device, mesh.shape["row"], mesh.shape["pair"]),
        mesh=mesh, in_specs=in_specs, out_specs=out_specs, check_vma=False,
    )
```

time: 148 us -> 34.8 us (0.24)
  blocking collectives: 49.2 us -> 0 us
  local copies, waits for them, and re-layouts: 46.9 us -> 4.85 us
  Pallas kernels: 0 us -> 25.8 us
  other arithmetic: 22.1 us -> 3.01 us
  starting transfers between devices: 18.8 us -> 0 us
  waiting for transfers between devices: 9.22 us -> 0 us
    psum x2 -> x0, blocking collectives: 49.2 us -> none  [the longest x1 42.1 us: on_device(): right_total = lax.psum(right_one, ('pair', 'row'))]
    pallas_call x0 -> x1, Pallas kernels: none -> 25.8 us  [on_device(): pl.pallas_call(functools.partial(body, sizes), out_shape=(jax.ShapeDtypeS...]
    slice x10 -> x0, local copies, waits for them, and re-layouts: 20.4 us -> none  [the longest x2 18.6 us: pool_field(): merged = merged[..., 0::2] + merged[..., 1::2]]
    ppermute x4 -> x0, starting transfers between devices: 12 us -> none  [the longest x2 9.44 us: padded_2(): lax.ppermute(lax.slice_in_dim(block, block.shape[dim] - width, None, axis...]
    div x11 -> x6, local copies, waits for them, and re-layouts: 12 us -> 0.45 us  [the longest x2 0.14 us: on_device(): left_one = spread_map(conv_map(left_two)) / 2.0 + left_sum / first_left]
    add x16 -> x10, other arithmetic: 9.26 us -> 1.56 us  [the longest x8 1.53 us: conv_map(): rows = padded[:, 0:n] + padded[:, 1:n + 1] + padded[:, 2:n + 2]]
    all_to_all x2 -> x0, waiting for transfers between devices: 7.42 us -> none  [the longest x1 3.97 us: on_device(): lax.all_to_all(pooled, 'row', split_axis=1, concat_axis=2, tiled=True)]
    all_to_all x2 -> x0, starting transfers between devices: 6.78 us -> none  [the longest x1 3.48 us: on_device(): lax.all_to_all(back_local, 'row', split_axis=2, concat_axis=1, tiled=True)]
  transfers between devices with their start and end apart: 6 -> 0, of which waited for: 4 -> 0; matrix products, arithmetic and copies ran while one was open for 3% -> 0% of each run, Pallas kernels for 0% -> 0%
where the time goes in v1:
time: 34.8 us; the launch traced here: 34.6 us
  Pallas kernels  25.8 us (74%)
  local copies, waits for them, and re-layouts  4.85 us (14%)
  other arithmetic  3.01 us (9%)
  between operations  0.92 us (3%)
    pallas_call x1, Pallas kernels, on_device(): pl.pallas_call(functools.partial(body, sizes), out_shape=(jax.ShapeDtypeS...  25.8 us
    unnamed x11, local copies, waits for them, and re-layouts  2.78 us
    add x8, other arithmetic, conv_map(): rows = padded[:, 0:n] + padded[:, 1:n + 1] + padded[:, 2:n + 2]  1.53 us
    div x3, other arithmetic, conv_map(): return (rows[:, :, 0:n] + rows[:, :, 1:n + 1] + rows[:, :, 2:n + 2]) / 9.0  0.73 us

profile of v1, /device:TPU:0, one launch (start us, length us, event | category | flops | bytes accessed | tf_op | source)
XLA Modules:
  0.0 34.6 jit_solution(7189220560771107936)
XLA Ops:
  0.6 1.0 %fusion.1 = f32[4,16,18]{2,1,0:T(8,128)S(1)} fusion(f32[4,16,16]{2,1,0:T(8,128)} %param.6), kind=kLoop, calls=%fused_computation.13 | loop fusion | flops 2304 | bytes 8704 | tf_op jit(solution)/shard_map/add | solution.py:19
  1.7 0.1 broadcast_in_dim.16.gl_ref
  1.9 0.1 broadcast_in_dim.17.il_ref
  2.0 0.2 copy.60
  2.2 0.1 reduce_sum.18
  2.3 0.1 copy.61
  2.5 0.1 rsqrt_multiply_fusion
  2.6 0.1 broadcast_in_dim.18.gl2_ref
  2.7 0.6 %copy-done.3 = f32[2,16,16]{2,1,0:T(8,128)S(1)} copy-done((f32[2,16,16]{2,1,0:T(8,128)S(1)}, f32[2,16,16]{2,1,0:T(8,128)}, u32[]{:S(2)}) %copy-start.3) | copy-done | bytes 2072
  3.4 0.1 fusion.7
  3.6 0.1 reshape.58
  3.7 0.1 reduce_sum.19
  4.0 0.1 reshape.59.gr2_ref
  4.2 0.1 reshape.55.gr_ref
  4.3 0.1 reshape.56.ir_ref
  4.4 0.1 broadcast_in_dim.19.il2_ref
  4.5 0.1 reshape.60.ir2_ref
  4.6 0.4 %copy-done.1 = f32[4,1,8,8,64]{4,3,2,1,0:T(8,128)S(1)} copy-done((f32[4,1,8,8,64]{4,3,2,1,0:T(8,128)S(1)}, f32[4,1,8,8,64]{4,3,2,1,0:T(8,128)}, u32[]{:S(2)}) %copy-start.1) | copy-done | bytes 65560
  5.1 25.8 %arc_reverse.1 = (f32[4,2,8,16,256]{4,3,2,1,0:T(8,128)S(1)}, f32[2,16,128]{2,1,0:T(8,128)S(1)}, f32[8,128]{1,0:T(8,128)S(1)}, f32[2,128]{1,0:T(2,128)S(1)}) custom-call(f32[4,2,8,16,256]{4,3,2,1,0:T(8,128)S(1)} %copy-done, f32[4,1,8,8,64]{4,3,2,1,0:T(8,128)S(1)} %copy-done.1, f32[4,8,16,128]{3,2,1,0:T(8,128)S(1)} %broadcast_in_dim.16.gl_ref, ...), custom_call_target="tpu_custom_call" | custom-call | tf_op jit(solution)/shard_map/arc_reverse/pallas_call | solution.py:472
  31.5 0.7 %copy.68 = f32[2,16,16]{2,1,0:T(8,128)} copy(f32[2,16,16]{1,2,0:T(8,128)S(1)} %fusion.14) | data formatting | bytes 4096
  32.4 0.1 fusion.15
  32.8 0.1 fusion.3
  32.9 0.7 %fusion.4 = f32[4,16,16]{2,1,0:T(8,128)} fusion(f32[4,16,18]{2,1,0:T(8,128)S(1)} %fusion.3), kind=kLoop, calls=%fused_computation.17 | loop fusion | flops 3072 | bytes 16384 | tf_op jit(solution)/shard_map/div | solution.py:20
  33.6 1.0 %copy.71 = f32[4,2,8,16,256]{4,3,2,1,0:T(8,128)} copy(f32[4,2,8,16,256]{4,3,2,1,0:T(8,128)S(1)} %get-tuple-element.38) | data formatting | bytes 2097152
  (47 shorter events, 1.8 us)
Async XLA Ops:
  1.7 2.9 %copy-start = (f32[4,2,8,16,256]{4,3,2,1,0:T(8,128)S(1)}, f32[4,2,8,16,256]{4,3,2,1,0:T(8,128)}, u32[]{:S(2)}) copy-start(f32[4,2,8,16,256]{4,3,2,1,0:T(8,128)} %gram_hbm.1) | copy-start | bytes 3145732
  2.6 0.7 %copy-start.3 = (f32[2,16,16]{2,1,0:T(8,128)S(1)}, f32[2,16,16]{2,1,0:T(8,128)}, u32[]{:S(2)}) copy-start(f32[2,16,16]{2,1,0:T(8,128)} %param.7) | copy-start | bytes 6148
  4.1 0.9 %copy-start.1 = (f32[4,1,8,8,64]{4,3,2,1,0:T(8,128)S(1)}, f32[4,1,8,8,64]{4,3,2,1,0:T(8,128)}, u32[]{:S(2)}) copy-start(f32[4,1,8,8,64]{4,3,2,1,0:T(8,128)} %cot_hbm.1) | copy-start | bytes 196612
  4.1 1.0 %copy-start.2 = (bf16[2,256,128]{2,1,0:T(8,128)(2,1)S(1)}, bf16[2,256,128]{2,1,0:T(8,128)(2,1)}, u32[]{:S(2)}) copy-start(bf16[2,256,128]{2,1,0:T(8,128)(2,1)} %constant.62.clone.mat_ref) | copy-start | bytes 393220

commit v2 on v1

v2 whole, which is shorter than its diff:
```python
import functools
import math

import jax
import jax.numpy as jnp
from jax import lax
from jax.experimental import pallas as pl
from jax.experimental.pallas import tpu as pltpu
from jax.sharding import PartitionSpec as P

ARCSIN_EVEN = (2.61397078, -1.36807576, 0.342139678, -0.0179491288)
ARCSIN_ROOT = (-1.61397053, 0.727749535, -0.104947558)


def divided(x, k):
    return x >> (k.bit_length() - 1) if k & (k - 1) == 0 else lax.div(x, k)


def left_over(x, k):
    return x & (k - 1) if k & (k - 1) == 0 else lax.rem(x, k)


def lane_of(shape):
    return lax.broadcasted_iota(jnp.int32, shape, len(shape) - 1)


def sub_of(shape):
    return lax.broadcasted_iota(jnp.int32, shape, len(shape) - 2)


def pool_matrix(length, group, t):
    half = length // 2
    shape = (length * length, group * half * half)
    row = sub_of(shape)
    lane = lane_of(shape)
    row_k, row_l = divided(row, length), left_over(row, length)
    lane_t, place = divided(lane, half * half), left_over(lane, half * half)
    same = (
        (lane_t == t)
        & (divided(row_k, 2) == divided(place, half))
        & (divided(row_l, 2) == left_over(place, half))
    )
    return jnp.where(same, 1.0, 0.0).astype(jnp.bfloat16)


def split_dot(x, matrix, dims=((1,), (0,)), terms=2):
    total = None
    for _ in range(terms):
        piece = x.astype(jnp.bfloat16)
        y = lax.dot_general(piece, matrix, (dims, ((), ())), preferred_element_type=jnp.float32)
        total = y if total is None else total + y
        x = x - piece.astype(jnp.float32)
    return total


def arc_parts(rho):
    square = rho * rho
    rest = 1.0 - square
    sine = rest * lax.rsqrt(rest)
    even = ARCSIN_EVEN[3]
    for c in ARCSIN_EVEN[2::-1]:
        even = even * square + c
    root = ARCSIN_ROOT[2]
    for c in ARCSIN_ROOT[1::-1]:
        root = root * square + c
    angle = (0.5 * math.pi) + rho * (even + sine * root)
    return sine, angle


def roll(x, shift, axis):
    return pltpu.roll(x, shift % x.shape[axis], axis)


def lane_masks(shape, side, chunks):
    lane = lane_of(shape)
    sub = sub_of(shape)
    col = left_over(lane, side)
    if chunks > 1:
        k_up, k_down = lane < 128 - side, lane >= side
    else:
        k = left_over(divided(lane, side), side)
        k_up, k_down = k + 1 < side, k >= 1
    l_up, l_down = col + 1 < side, col >= 1
    return k_up, k_down, l_up, l_down, l_up & (sub + 1 < shape[0]), l_down & (sub >= 1)


def shift_k_up(chunks, side, mask):
    rolled = [roll(c, -side, 1) for c in chunks] + [0.0]
    return [jnp.where(mask, rolled[h], rolled[h + 1]) for h in range(len(chunks))]


def shift_k_down(chunks, side, mask):
    rolled = [0.0] + [roll(c, side, 1) for c in chunks]
    return [jnp.where(mask, rolled[h + 1], rolled[h]) for h in range(len(chunks))]


def conv_rows(rows, side, masks):
    k_up, k_down, _, _, v_up, v_down = masks
    out = []
    for i in range(1, len(rows) - 1):
        inner = rows[i]
        if rows[i + 1] is not None:
            inner = [x + y for x, y in zip(inner, shift_k_up(rows[i + 1], side, k_up))]
        if rows[i - 1] is not None:
            inner = [x + y for x, y in zip(inner, shift_k_down(rows[i - 1], side, k_down))]
        done = []
        for x in inner:
            up = jnp.where(v_up, roll(roll(x, -1, 0), -1, 1), 0.0)
            down = jnp.where(v_down, roll(roll(x, 1, 0), 1, 1), 0.0)
            done.append(x + up + down)
        out.append(done)
    return out


def conv_flat(chunks, side, masks):
    k_up, k_down, l_up, l_down, _, _ = masks
    ups = shift_k_up(chunks, side, k_up)
    downs = shift_k_down(chunks, side, k_down)
    out = []
    for x, up, down in zip(chunks, ups, downs):
        x = x + up + down
        x = x + jnp.where(l_up, roll(x, -1, 1), 0.0) + jnp.where(l_down, roll(x, 1, 1), 0.0)
        out.append(x * (1.0 / 9.0))
    return out


def conv_columns(columns):
    count, extent = columns.shape[0], columns.shape[1]
    sub = sub_of((extent, 128))
    out = []
    for i in range(count):
        x = columns[i]
        if i > 0:
            x = x + columns[i - 1]
        if i + 1 < count:
            x = x + columns[i + 1]
        up = jnp.where(sub + 1 < extent, roll(x, -1, 0), 0.0)
        down = jnp.where(sub >= 1, roll(x, 1, 0), 0.0)
        out.append((x + up + down) * (1.0 / 9.0))
    return out


def root_pair(x):
    inverse = lax.rsqrt(x)
    return x * inverse, inverse


def rounded(count):
    return -(-count // 8) * 8


def body(
    sizes,
    gram_hbm, cot_hbm, lv_ref, rv_ref,
    out_hbm, left_out, right_out,
    gram, cot, slope, sinem, kp, tmp, pooled, back, fine, wsum, wsum2, racc, out_v, packet, pair_all, pair_packet,
    gl_ref, il_ref, gl2_ref, il2_ref, gr_ref, ir_ref, gr2_ref, ir2_ref, mat_ref, lmap, cols, half_cols, ccol,
    load_sem, out_sem, halo_send, halo_recv, cot_send, cot_recv, pool_send, pool_recv,
    slope_send, slope_recv, left_send, left_recv, pair_send, pair_recv,
):
    n, npair, A, B, rows, R, group, part = sizes
    H = R // 2
    W = R * R
    NH = W // 128
    G = B // group
    PR = rows // 2
    Bp = rounded(B)
    Gp = rounded(G)
    LR = A * rows
    me = lax.axis_index("row")
    mine = lax.axis_index("pair")
    f32 = jnp.float32

    def chunk(h):
        return slice(h * 128, (h + 1) * 128)

    barrier = pltpu.get_barrier_semaphore()
    for d in range(1, n):
        pl.semaphore_signal(barrier, inc=1, device_id={"row": lax.rem(me + d, n)})
    for d in range(1, npair):
        pl.semaphore_signal(barrier, inc=1, device_id={"pair": lax.rem(mine + d, npair)})

    loads = []
    for a in range(A):
        c = pltpu.make_async_copy(gram_hbm.at[a], gram.at[a, :, pl.ds(1, rows)], load_sem.at[a])
        c.start()
        loads.append(c)
    cot_load = pltpu.make_async_copy(cot_hbm, cot.at[me], load_sem.at[A])
    cot_load.start()

    pl.semaphore_wait(barrier, n - 1 + npair - 1)

    has_low = me > 0
    has_high = me < n - 1
    low = jnp.maximum(me - 1, 0)
    high = jnp.minimum(me + 1, n - 1)

    def halo_up():
        return pltpu.make_async_remote_copy(
            src_ref=gram_hbm.at[:, :, rows - 1], dst_ref=gram.at[:, :, 0],
            send_sem=halo_send.at[0], recv_sem=halo_recv.at[0], device_id={"row": high})

    def halo_down():
        return pltpu.make_async_remote_copy(
            src_ref=gram_hbm.at[:, :, 0], dst_ref=gram.at[:, :, rows + 1],
            send_sem=halo_send.at[1], recv_sem=halo_recv.at[1], device_id={"row": low})

    def slope_up():
        return pltpu.make_async_remote_copy(
            src_ref=slope.at[:, :, rows], dst_ref=slope.at[:, :, 0],
            send_sem=slope_send.at[0], recv_sem=slope_recv.at[0], device_id={"row": high})

    def slope_down():
        return pltpu.make_async_remote_copy(
            src_ref=slope.at[:, :, 1], dst_ref=slope.at[:, :, rows + 1],
            send_sem=slope_send.at[1], recv_sem=slope_recv.at[1], device_id={"row": low})

    def row_copy(ref, sends, recvs, d):
        return pltpu.make_async_remote_copy(
            src_ref=ref.at[me], dst_ref=ref.at[me], send_sem=sends.at[d],
            recv_sem=recvs.at[me], device_id={"row": lax.rem(me + d, n)})

    def row_arrival(ref, sends, recvs, d):
        source = lax.rem(me + d, n)
        return pltpu.make_async_remote_copy(
            src_ref=ref.at[source], dst_ref=ref.at[source], send_sem=sends.at[d],
            recv_sem=recvs.at[source], device_id={"row": source})

    def pool_copy(d, a):
        return pltpu.make_async_remote_copy(
            src_ref=pooled.at[me, a], dst_ref=pooled.at[me, a], send_sem=pool_send.at[d, a],
            recv_sem=pool_recv.at[me, a], device_id={"row": lax.rem(me + d, n)})

    def pool_arrival(d, a):
        source = lax.rem(me + d, n)
        return pltpu.make_async_remote_copy(
            src_ref=pooled.at[source, a], dst_ref=pooled.at[source, a], send_sem=pool_send.at[d, a],
            recv_sem=pool_recv.at[source, a], device_id={"row": source})

    @pl.when(has_high)
    def _():
        halo_up().start()

    @pl.when(has_low)
    def _():
        halo_down().start()

    cot_load.wait()
    for d in range(1, n):
        row_copy(cot, cot_send, cot_recv, d).start()

    zero_row = jnp.zeros((A, B, R, W), f32)

    @pl.when(jnp.logical_not(has_low))
    def _():
        gram[:, :, 0] = zero_row
        slope[:, :, 0] = zero_row

    @pl.when(jnp.logical_not(has_high))
    def _():
        gram[:, :, rows + 1] = zero_row
        slope[:, :, rows + 1] = zero_row

    for t in range(group):
        mat_ref[t] = pool_matrix(R, group, t)
    ones = jnp.ones((128, 128), jnp.bfloat16)
    lmap[...] = jnp.zeros((A, R, 128), f32)
    lmap[:, :, 0:R] = lv_ref[...]
    sub16 = sub_of((R, 128))
    lane16 = lane_of((R, 128))
    band = jnp.abs(sub16 - lane16) <= 1
    for a in range(A):
        v = lmap[a]
        v = v + jnp.where(sub16 + 1 < R, roll(v, -1, 0), 0.0) + jnp.where(sub16 >= 1, roll(v, 1, 0), 0.0)
        lmap[a] = v
        for i in range(R):
            line = jnp.broadcast_to(lmap[a, i : i + 1, :], (R, 128))
            cols[a, i] = jnp.where(band, line, 0.0)
        spread = split_dot(cols[a].reshape(R * R, 128), ones, terms=3) * (1.0 / 9.0)
        cols[a] = spread.reshape(R, R, 128)
        for c in range(H):
            half_cols[a, c * R : (c + 1) * R] = cols[a, 2 * c] + cols[a, 2 * c + 1]
        even = half_cols[a, pl.ds(0, H * H, stride=2), :]
        odd = half_cols[a, pl.ds(1, H * H, stride=2), :]
        second = conv_columns(((even + odd) * 0.125).reshape(H, H, 128))
        for i in range(H):
            g2, i2 = root_pair(second[i])
            gl2_ref[a, i] = g2
            il2_ref[a, i] = i2 * (1.0 / 9.0)
        g1, i1 = root_pair(cols[a, pl.ds(me * rows, rows)])
        gl_ref[a] = g1
        il_ref[a] = i1 * (1.0 / 9.0)

    flat_masks = lane_masks((Bp, 128), R, NH)
    flat_masks2 = lane_masks((Gp, 128), H, 1)
    first_right = conv_flat([rv_ref[:, chunk(h)] for h in range(NH)], R, flat_masks)
    for h in range(NH):
        gr_ref[:, chunk(h)], ir_ref[:, chunk(h)] = root_pair(first_right[h])
    first_flat = jnp.concatenate(first_right, axis=1)
    small = [split_dot(first_flat, mat_ref[t], terms=3) for t in range(group)]
    gr2_ref[...] = jnp.ones((Gp, 128), f32)
    for g in range(G):
        line = None
        for t in range(group):
            b = g * group + t
            y = small[t][b : b + 1, :]
            line = y if line is None else line + y
        gr2_ref[g : g + 1, :] = line * 0.125
    (second_right,) = conv_flat([gr2_ref[...]], H, flat_masks2)
    gr2_ref[...], ir2_ref[...] = root_pair(second_right)

    for c in loads:
        c.wait()

    masks = lane_masks((R, 128), R, NH)

    def forward(a, b, p):
        f = [[gram[a, b, 2 * p + t, :, chunk(h)] for h in range(NH)] for t in range(4)]
        source = conv_rows(f, R, masks)
        for h in range(NH):
            total = None
            for t in range(2):
                i = 2 * p + t
                m = gl_ref[a, i] * gr_ref[b : b + 1, chunk(h)]
                rho = source[t][h] * (il_ref[a, i] * ir_ref[b : b + 1, chunk(h)])
                sine, angle = arc_parts(rho)
                sm = m * sine
                slope[a, b, i + 1, :, chunk(h)] = angle
                sinem[a, b, i, :, chunk(h)] = sm
                term = sm + m * (angle * rho)
                total = term if total is None else total + term
            kp[a, b, p, :, chunk(h)] = total

    interior = list(range(1, PR - 1))
    edges = sorted({0, PR - 1})

    if interior:
        @pl.loop(0, A)
        def _(a):
            for b in range(B):
                for p in interior:
                    forward(a, b, p)

    @pl.when(has_low)
    def _():
        halo_up().wait_recv()

    @pl.when(has_high)
    def _():
        halo_down().wait_recv()

    @pl.loop(0, A)
    def _(a):
        for b in range(B):
            for p in edges:
                forward(a, b, p)
        for g in range(G):
            acc = None
            for t in range(group):
                y = split_dot(kp[a, g * group + t].reshape(PR * R, W), mat_ref[t])
                acc = y if acc is None else acc + y
            tmp[g, 0 : PR * R] = acc
            even = tmp[g, pl.ds(0, PR * H, stride=2), :]
            odd = tmp[g, pl.ds(1, PR * H, stride=2), :]
            pooled[me, a, g] = ((even + odd) * (1.0 / (32.0 * math.pi))).reshape(PR, H, 128)
        for d in range(1, n):
            pool_copy(d, a).start()

    @pl.when(has_high)
    def _():
        slope_up().start()

    @pl.when(has_low)
    def _():
        slope_down().start()

    for d in range(1, n):
        row_arrival(cot, cot_send, cot_recv, d).wait_recv()

    masks2 = lane_masks((H, 128), H, 1)
    racc[...] = jnp.zeros((NH * B + G, R, 128), f32)

    @pl.loop(0, A)
    def _(a):
        for d in range(1, n):
            pool_arrival(d, a).wait_recv()
        left2 = [None] * H
        for g in range(G):
            f = [None] + [[pooled[i // PR, a, g, i % PR]] for i in range(H)] + [None]
            source = conv_rows(f, H, masks2)
            ct = [None]
            right2 = None
            for i in range(H):
                m = gl2_ref[a, i] * gr2_ref[g : g + 1, :]
                rho = source[i][0] * (il2_ref[a, i] * ir2_ref[g : g + 1, :])
                sine, angle = arc_parts(rho)
                pieces = []
                for t in range(group):
                    b = g * group + t
                    pieces.append(cot[b // part, a, b % part, i])
                c = jnp.concatenate(pieces, axis=1)
                ct.append([c * angle])
                w = c * (m * sine)
                right2 = w if right2 is None else right2 + w
                left2[i] = w if left2[i] is None else left2[i] + w
            ct.append(None)
            racc[NH * B + g, 0:H] = racc[NH * B + g, 0:H] + right2
            b_rows = conv_rows(ct, H, masks2)
            scale = 1.0 / (9.0 * 2.0 * math.pi * 16.0) / (18.0 * math.pi)
            zero = jnp.zeros((H, 128), f32)
            back[g, 0] = zero
            back[g, H + 1] = zero
            for i in range(H):
                back[g, i + 1] = b_rows[i][0] * scale
            x = back[g, pl.ds(me * PR, PR + 2)].reshape((PR + 2) * H, 128)
            for t in range(group):
                y = split_dot(x, mat_ref[t], ((1,), (1,)))
                for h in range(NH):
                    fine[a, g * group + t, h, pl.ds(0, (PR + 2) * H, stride=2), :] = y[:, chunk(h)]
                    fine[a, g * group + t, h, pl.ds(1, (PR + 2) * H, stride=2), :] = y[:, chunk(h)]
        for i in range(H):
            wsum2[a, i] = left2[i]

        lsum = [None] * rows
        for b in range(B):
            for h in range(NH):
                total = None
                for p in range(PR):
                    bk = fine[a, b, h, (p + 1) * R : (p + 2) * R, :]
                    for t in range(2):
                        i = 2 * p + t
                        w = bk * sinem[a, b, i, :, chunk(h)]
                        total = w if total is None else total + w
                        lsum[i] = w if lsum[i] is None else lsum[i] + w
                racc[h * B + b] = racc[h * B + b] + total
        for i in range(rows):
            wsum[a, i] = lsum[i]

    diagonal = (sub16 == lane16)[None]
    sums = split_dot(wsum[...].reshape(LR * R, 128), ones).reshape(LR, R, 128)
    inverse = il_ref[...].reshape(LR, R, 128)
    sums = sums * (inverse * inverse * (4.5 * 81.0))
    packet[me, 0:LR, :] = jnp.sum(jnp.where(diagonal, sums, 0.0), axis=1)
    right_sums = jnp.sum(racc[...], axis=1)
    packet[me, LR : LR + NH * B, :] = right_sums[0 : NH * B]
    for d in range(1, n):
        row_copy(packet, left_send, left_recv, d).start()

    def final(a, b, chosen):
        cache = {}

        def product(i):
            if i not in cache:
                c = (i + 1) // 2
                cache[i] = [
                    fine[a, b, h, c * R : (c + 1) * R, :] * slope[a, b, i, :, chunk(h)] for h in range(NH)
                ]
            return cache[i]

        for i in chosen:
            (value,) = conv_rows([product(i - 1), product(i), product(i + 1)], R, masks)
            for h in range(NH):
                out_v[a, b, i - 1, :, chunk(h)] = value[h]

    def inner_out(a):
        inner = pl.ds(1, rows - 2)
        return pltpu.make_async_copy(out_v.at[a, :, inner], out_hbm.at[a, :, inner], out_sem.at[0, a])

    def edge_out(a, i, s):
        return pltpu.make_async_copy(out_v.at[a, :, i], out_hbm.at[a, :, i], out_sem.at[s, a])

    if rows > 2:
        @pl.loop(0, A)
        def _(a):
            for b in range(B):
                final(a, b, range(2, rows))
            inner_out(a).start()

    for d in range(1, n):
        row_arrival(packet, left_send, left_recv, d).wait_recv()
    right = packet[0, LR : LR + NH * B, :]
    for r in range(1, n):
        right = right + packet[r, LR : LR + NH * B, :]
    pair_packet[...] = jnp.zeros(pair_packet.shape, f32)
    pair_packet[0 : NH * B, :] = right
    pair_packet[NH * B : NH * B + G, :] = right_sums[NH * B : NH * B + G]
    pair_all[mine] = pair_packet[...]

    def pair_copy(d):
        return pltpu.make_async_remote_copy(
            src_ref=pair_packet, dst_ref=pair_all.at[mine], send_sem=pair_send.at[d],
            recv_sem=pair_recv.at[mine], device_id={"pair": lax.rem(mine + d, npair)})

    def pair_arrival(d):
        source = lax.rem(mine + d, npair)
        return pltpu.make_async_remote_copy(
            src_ref=pair_packet, dst_ref=pair_all.at[source], send_sem=pair_send.at[d],
            recv_sem=pair_recv.at[source], device_id={"pair": source})

    for d in range(1, npair):
        pair_copy(d).start()

    @pl.when(has_low)
    def _():
        slope_up().wait_recv()

    @pl.when(has_high)
    def _():
        slope_down().wait_recv()

    @pl.loop(0, A)
    def _(a):
        for b in range(B):
            final(a, b, sorted({1, rows}))
        edge_out(a, 0, 1).start()
        edge_out(a, rows - 1, 2).start()

    inverse2 = il2_ref[...].reshape(A * H, H, 128)
    sums2 = split_dot(wsum2[...].reshape(A * H * H, 128), ones).reshape(A * H, H, 128)
    sums2 = sums2 * (inverse2 * inverse2 * (81.0 / (4.0 * math.pi * 8.0)))
    for a in range(A):
        mixed = conv_columns(sums2[a * H : (a + 1) * H])
        for c in range(H):
            for t in range(2):
                ccol[pl.ds((2 * c + t) * R, H, stride=2), :] = mixed[c]
                ccol[pl.ds((2 * c + t) * R + 1, H, stride=2), :] = mixed[c]
        coarse = jnp.sum(jnp.where(diagonal, ccol[...].reshape(R, R, 128), 0.0), axis=1)
        local = jnp.concatenate([packet[r, a * rows : (a + 1) * rows, :] for r in range(n)], axis=0)
        v = coarse + local
        v = v + jnp.where(sub16 + 1 < R, roll(v, -1, 0), 0.0) + jnp.where(sub16 >= 1, roll(v, 1, 0), 0.0)
        v = (v + roll(v, 1, 1) + roll(v, -1, 1)) * (1.0 / 9.0)
        left_out[a] = v[:, 0:R]

    for d in range(1, npair):
        pair_arrival(d).wait_recv()
    total = pair_all[0]
    for r in range(1, npair):
        total = total + pair_all[r]
    pair_packet_rows = pair_packet.shape[0]
    tmp[0, 0:pair_packet_rows, :] = total
    tmp[0, pair_packet_rows : pair_packet_rows + Gp, :] = jnp.zeros((Gp, 128), f32)
    coarse = tmp[0, NH * B : NH * B + Gp, :]
    (coarse,) = conv_flat([coarse * (ir2_ref[...] * ir2_ref[...] * (1.0 / (4.0 * math.pi * 8.0)))], H, flat_masks2)
    wide = [split_dot(coarse, mat_ref[t], ((1,), (1,)), terms=3) for t in range(group)]
    for b in range(B):
        right_out[b : b + 1, :] = wide[b % group][b // group : b // group + 1, :]
    if Bp > B:
        right_out[B:Bp, :] = jnp.zeros((Bp - B, W), f32)
    pieces = []
    for h in range(NH):
        scale = ir_ref[:, chunk(h)]
        pieces.append(right_out[:, chunk(h)] + tmp[0, h * B : h * B + Bp, :] * (scale * scale * 4.5))
    pieces = conv_flat(pieces, R, flat_masks)
    for h in range(NH):
        right_out[:, chunk(h)] = pieces[h]

    for a in range(A):
        if rows > 2:
            inner_out(a).wait()
        edge_out(a, 0, 1).wait()
        edge_out(a, rows - 1, 2).wait()

    @pl.when(has_high)
    def _():
        halo_up().wait_send()
        slope_up().wait_send()

    @pl.when(has_low)
    def _():
        halo_down().wait_send()
        slope_down().wait_send()

    for d in range(1, n):
        row_copy(cot, cot_send, cot_recv, d).wait_send()
        row_copy(packet, left_send, left_recv, d).wait_send()
        for a in range(A):
            pool_copy(d, a).wait_send()
    for d in range(1, npair):
        pair_copy(d).wait_send()


def on_device(n, npair, gram_field, left_variance, right_variance, cotangent):
    A, B, rows, R, W = gram_field.shape
    part = cotangent.shape[1]
    H = R // 2
    NH = W // 128
    width = H * H
    group = 128 // width
    G = B // group
    PR = rows // 2
    Bp, Gp = rounded(B), rounded(G)
    f32 = jnp.float32
    right_flat = jnp.pad(right_variance.reshape(B, W), ((0, Bp - B), (0, 0)), constant_values=1.0)

    pair_rows = rounded(NH * B + G)
    packet_rows = rounded(A * rows + NH * B)
    sizes = (n, npair, A, B, rows, R, group, part)
    vmem = pl.BlockSpec(memory_space=pltpu.VMEM)
    hbm = pl.BlockSpec(memory_space=pl.ANY)
    dma = pltpu.SemaphoreType.DMA

    def scratch(*shape):
        return pltpu.VMEM(shape, f32)

    out, left, right = pl.pallas_call(
        functools.partial(body, sizes),
        out_shape=(
            jax.ShapeDtypeStruct(gram_field.shape, f32),
            jax.ShapeDtypeStruct((A, R, R), f32),
            jax.ShapeDtypeStruct((Bp, W), f32),
        ),
        in_specs=[hbm, hbm, vmem, vmem],
        out_specs=(hbm, vmem, vmem),
        scratch_shapes=[
            scratch(A, B, rows + 2, R, W),
            scratch(n, A, part, H, H, width),
            scratch(A, B, rows + 2, R, W),
            scratch(A, B, rows, R, W),
            scratch(A, B, PR, R, W),
            scratch(G, max(PR * R, pair_rows + Gp, NH * B + Bp), 128),
            scratch(n, A, G, PR, H, 128),
            scratch(G, H + 2, H, 128),
            scratch(A, B, NH, (PR + 2) * R, 128),
            scratch(A, rows, R, 128),
            scratch(A, H, H, 128),
            scratch(NH * B + G, R, 128),
            scratch(A, B, rows, R, W),
            scratch(n, packet_rows, 128),
            scratch(npair, pair_rows, 128),
            scratch(pair_rows, 128),
            scratch(A, rows, R, 128),
            scratch(A, rows, R, 128),
            scratch(A, H, H, 128),
            scratch(A, H, H, 128),
            scratch(Bp, W),
            scratch(Bp, W),
            scratch(Gp, 128),
            scratch(Gp, 128),
            pltpu.VMEM((group, W, 128), jnp.bfloat16),
            scratch(A, R, 128),
            scratch(A, R, R, 128),
            scratch(A, H * R, 128),
            scratch(R * R, 128),
            dma((A + 1,)), dma((3, A)), dma((2,)), dma((2,)),
            dma((n,)), dma((n,)), dma((n, A)), dma((n, A)),
            dma((2,)), dma((2,)), dma((n,)), dma((n,)), dma((npair,)), dma((npair,)),
        ],
        compiler_params=pltpu.CompilerParams(
            collective_id=0, has_side_effects=True, vmem_limit_bytes=48 * 1024 * 1024
        ),
        name="arc_reverse",
    )(gram_field, cotangent, left_variance, right_flat)
    return out, left, right[:B].reshape(B, R, R)


def solution(mesh):
    in_specs = (
        P("pair", None, "row", None, None),
        P("pair", None, None),
        P(),
        P("pair", "row", None, None, None),
    )
    out_specs = (P("pair", None, "row", None, None), P("pair", None, None), P())
    return jax.shard_map(
        functools.partial(on_device, mesh.shape["row"], mesh.shape["pair"]),
        mesh=mesh, in_specs=in_specs, out_specs=out_specs, check_vma=False,
    )
```

time: 34.8 us -> 31.1 us (0.89)
  other arithmetic: 3.01 us -> 0 us
  Pallas kernels: 25.8 us -> 24.2 us
  local copies, waits for them, and re-layouts: 4.85 us -> 5.96 us
    unnamed x11 -> x8, local copies, waits for them, and re-layouts: 2.78 us -> 4.46 us
    pallas_call x1, Pallas kernels: 25.8 us -> 24.2 us  [on_device(): pl.pallas_call(functools.partial(body, sizes), out_shape=(jax.ShapeDtypeS...]
    add x10 -> x0, other arithmetic: 1.56 us -> none  [the longest x8 1.53 us: conv_map(): rows = padded[:, 0:n] + padded[:, 1:n + 1] + padded[:, 2:n + 2]]
    div x15 -> x0, other arithmetic: 1.15 us -> none  [the longest x3 0.73 us: conv_map(): return (rows[:, :, 0:n] + rows[:, :, 1:n + 1] + rows[:, :, 2:n + 2]) / 9.0]
    reshape x5 -> x2, local copies, waits for them, and re-layouts: 0.45 us -> 1.49 us  [the longest x1 0.8 us: on_device(): right_variance.reshape(B, W)]
    div x7 -> x0, local copies, waits for them, and re-layouts: 0.62 us -> none  [the longest x1 0.17 us: on_device(): second_left = conv_map(pool_map(first_left / 2.0))]
    broadcast_in_dim x8 -> x0, local copies, waits for them, and re-layouts: 0.49 us -> none  [the longest x1 0.13 us: on_device(): jnp.broadcast_to((lax.rsqrt(my_left) / 9.0)[..., None], (A, rows, R, 128))]
where the time goes in v2:
time: 31.1 us; the launch traced here: 30.8 us
  Pallas kernels  24.2 us (78%)
  local copies, waits for them, and re-layouts  5.96 us (19%)
  between operations  0.66 us (2%)
    pallas_call x1, Pallas kernels, on_device(): pl.pallas_call(functools.partial(body, sizes), out_shape=(jax.ShapeDtypeS...  24.2 us
    unnamed x8, local copies, waits for them, and re-layouts  4.46 us
    reshape x1, local copies, waits for them, and re-layouts, on_device(): right_variance.reshape(B, W)  0.8 us
    reshape x1, local copies, waits for them, and re-layouts, on_device(): return (out, left, right[:B].reshape(B, R, R))  0.69 us

profile of v2, /device:TPU:0, one launch (start us, length us, event | category | flops | bytes accessed | tf_op | source)
XLA Modules:
  0.0 30.8 jit_solution(3385177474868923260)
XLA Ops:
  0.6 0.8 %reshape.12 = f32[2,256]{1,0:T(2,128)S(1)} reshape(f32[2,16,16]{2,1,0:T(8,128)} %param.6) | data formatting | bytes 4096 | tf_op jit(solution)/shard_map/reshape | solution.py:593
  1.4 0.0 copy-start
  1.4 1.2 %copy-done = f32[4,2,8,16,256]{4,3,2,1,0:T(8,128)S(1)} copy-done((f32[4,2,8,16,256]{4,3,2,1,0:T(8,128)S(1)}, f32[4,2,8,16,256]{4,3,2,1,0:T(8,128)}, u32[]{:S(2)}) %copy-start) | copy-done | bytes 1048600
  2.7 0.0 copy-start.1
  2.7 0.9 %copy-done.1 = f32[4,1,8,8,64]{4,3,2,1,0:T(8,128)S(1)} copy-done((f32[4,1,8,8,64]{4,3,2,1,0:T(8,128)S(1)}, f32[4,1,8,8,64]{4,3,2,1,0:T(8,128)}, u32[]{:S(2)}) %copy-start.1) | copy-done | bytes 65560
  3.6 0.0 copy-start.2
  3.6 0.8 %copy-done.2 = f32[4,16,16]{2,1,0:T(8,128)S(1)} copy-done((f32[4,16,16]{2,1,0:T(8,128)S(1)}, f32[4,16,16]{2,1,0:T(8,128)}, u32[]{:S(2)}) %copy-start.2) | copy-done | bytes 4120
  4.3 24.2 %arc_reverse.1 = (f32[4,2,8,16,256]{4,3,2,1,0:T(8,128)S(1)}, f32[4,16,16]{2,1,0:T(8,128)S(1)}, f32[8,256]{1,0:T(8,128)S(1)}) custom-call(f32[4,2,8,16,256]{4,3,2,1,0:T(8,128)S(1)} %copy-done, f32[4,1,8,8,64]{4,3,2,1,0:T(8,128)S(1)} %copy-done.1, f32[4,16,16]{2,1,0:T(8,128)S(1)} %copy-done.2, f32[8,256]{1,0:T(8,128)S(1)} %pad.4.rv_ref), custom_call_target="tpu_custom_call" | custom-call | tf_op jit(solution)/shard_map/arc_reverse/pallas_call | solution.py:605
  28.6 0.7 %reshape.13 = f32[2,16,16]{2,1,0:T(8,128)} reshape(f32[2,256]{1,0:T(2,128)S(1)} %slice.3) | data formatting | bytes 4096 | tf_op jit(solution)/shard_map/reshape | solution.py:653
  29.2 1.0 %copy.9 = f32[4,2,8,16,256]{4,3,2,1,0:T(8,128)} copy(f32[4,2,8,16,256]{4,3,2,1,0:T(8,128)S(1)} %get-tuple-element.12) | data formatting | bytes 2097152
  30.2 0.6 %copy.10 = f32[4,16,16]{2,1,0:T(8,128)} copy(f32[4,16,16]{2,1,0:T(8,128)S(1)} %get-tuple-element.13) | data formatting | bytes 8192
  (2 shorter events, 0.0 us)
Async XLA Ops:
  1.4 1.2 %copy-start = (f32[4,2,8,16,256]{4,3,2,1,0:T(8,128)S(1)}, f32[4,2,8,16,256]{4,3,2,1,0:T(8,128)}, u32[]{:S(2)}) copy-start(f32[4,2,8,16,256]{4,3,2,1,0:T(8,128)} %gram_hbm.1) | copy-start | bytes 3145732
  2.7 0.9 %copy-start.1 = (f32[4,1,8,8,64]{4,3,2,1,0:T(8,128)S(1)}, f32[4,1,8,8,64]{4,3,2,1,0:T(8,128)}, u32[]{:S(2)}) copy-start(f32[4,1,8,8,64]{4,3,2,1,0:T(8,128)} %cot_hbm.1) | copy-start | bytes 196612
  3.6 0.8 %copy-start.2 = (f32[4,16,16]{2,1,0:T(8,128)S(1)}, f32[4,16,16]{2,1,0:T(8,128)}, u32[]{:S(2)}) copy-start(f32[4,16,16]{2,1,0:T(8,128)} %lv_ref.1) | copy-start | bytes 12292

commit v3 on v2

--- a/solution.py
+++ b/solution.py
@@ -151,11 +151,12 @@
 
 def body(
     sizes,
-    gram_hbm, cot_hbm, lv_ref, rv_ref,
-    out_hbm, left_out, right_out,
-    gram, cot, slope, sinem, kp, tmp, pooled, back, fine, wsum, wsum2, racc, out_v, packet, pair_all, pair_packet,
+    gram_hbm, cot_hbm, lv_hbm, rv_hbm,
+    out_v, left_out, right_out,
+    gram, cot, slope, sinem, kp, tmp, pooled, back, fine, wsum, wsum2, racc, packet, pair_all, pair_packet,
     gl_ref, il_ref, gl2_ref, il2_ref, gr_ref, ir_ref, gr2_ref, ir2_ref, mat_ref, lmap, cols, half_cols, ccol,
-    load_sem, out_sem, halo_send, halo_recv, cot_send, cot_recv, pool_send, pool_recv,
+    lv_ref, rv_ref, right_flat,
+    load_sem, halo_send, halo_recv, cot_send, cot_recv, pool_send, pool_recv,
     slope_send, slope_recv, left_send, left_recv, pair_send, pair_recv,
 ):
     n, npair, A, B, rows, R, group, part = sizes
@@ -187,6 +188,10 @@
         loads.append(c)
     cot_load = pltpu.make_async_copy(cot_hbm, cot.at[me], load_sem.at[A])
     cot_load.start()
+    left_load = pltpu.make_async_copy(lv_hbm, lv_ref, load_sem.at[A + 1])
+    left_load.start()
+    right_load = pltpu.make_async_copy(rv_hbm, rv_ref, load_sem.at[A + 2])
+    right_load.start()
 
     pl.semaphore_wait(barrier, n - 1 + npair - 1)
 
@@ -226,17 +231,6 @@
             src_ref=ref.at[source], dst_ref=ref.at[source], send_sem=sends.at[d],
             recv_sem=recvs.at[source], device_id={"row": source})
 
-    def pool_copy(d, a):
-        return pltpu.make_async_remote_copy(
-            src_ref=pooled.at[me, a], dst_ref=pooled.at[me, a], send_sem=pool_send.at[d, a],
-            recv_sem=pool_recv.at[me, a], device_id={"row": lax.rem(me + d, n)})
-
-    def pool_arrival(d, a):
-        source = lax.rem(me + d, n)
-        return pltpu.make_async_remote_copy(
-            src_ref=pooled.at[source, a], dst_ref=pooled.at[source, a], send_sem=pool_send.at[d, a],
-            recv_sem=pool_recv.at[source, a], device_id={"row": source})
-
     @pl.when(has_high)
     def _():
         halo_up().start()
@@ -264,6 +258,8 @@
     for t in range(group):
         mat_ref[t] = pool_matrix(R, group, t)
     ones = jnp.ones((128, 128), jnp.bfloat16)
+    left_load.wait()
+    right_load.wait()
     lmap[...] = jnp.zeros((A, R, 128), f32)
     lmap[:, :, 0:R] = lv_ref[...]
     sub16 = sub_of((R, 128))
@@ -273,13 +269,16 @@
         v = lmap[a]
         v = v + jnp.where(sub16 + 1 < R, roll(v, -1, 0), 0.0) + jnp.where(sub16 >= 1, roll(v, 1, 0), 0.0)
         lmap[a] = v
+    for a in range(A):
         for i in range(R):
             line = jnp.broadcast_to(lmap[a, i : i + 1, :], (R, 128))
             cols[a, i] = jnp.where(band, line, 0.0)
-        spread = split_dot(cols[a].reshape(R * R, 128), ones, terms=3) * (1.0 / 9.0)
-        cols[a] = spread.reshape(R, R, 128)
+    spread = split_dot(cols[...].reshape(A * R * R, 128), ones, terms=3) * (1.0 / 9.0)
+    cols[...] = spread.reshape(A, R, R, 128)
+    for a in range(A):
         for c in range(H):
             half_cols[a, c * R : (c + 1) * R] = cols[a, 2 * c] + cols[a, 2 * c + 1]
+    for a in range(A):
         even = half_cols[a, pl.ds(0, H * H, stride=2), :]
         odd = half_cols[a, pl.ds(1, H * H, stride=2), :]
         second = conv_columns(((even + odd) * 0.125).reshape(H, H, 128))
@@ -293,7 +292,18 @@
 
     flat_masks = lane_masks((Bp, 128), R, NH)
     flat_masks2 = lane_masks((Gp, 128), H, 1)
-    first_right = conv_flat([rv_ref[:, chunk(h)] for h in range(NH)], R, flat_masks)
+    wide_lane = lane_of((R, W))
+    here = divided(wide_lane, R) == sub_of((R, W))
+    choose = jnp.where(
+        left_over(sub_of((W, 128)), R) == lane_of((W, 128)), 1.0, 0.0
+    ).astype(jnp.bfloat16)
+    right_flat[...] = jnp.ones((Bp, W), f32)
+    for b in range(B):
+        lmap[0] = jnp.zeros((R, 128), f32)
+        lmap[0, :, 0:R] = rv_ref[b]
+        tiled = split_dot(lmap[0], choose, ((1,), (1,)), terms=3)
+        right_flat[b : b + 1, :] = jnp.sum(jnp.where(here, tiled, 0.0), axis=0, keepdims=True)
+    first_right = conv_flat([right_flat[:, chunk(h)] for h in range(NH)], R, flat_masks)
     for h in range(NH):
         gr_ref[:, chunk(h)], ir_ref[:, chunk(h)] = root_pair(first_right[h])
     first_flat = jnp.concatenate(first_right, axis=1)
@@ -329,13 +339,13 @@
                 sinem[a, b, i, :, chunk(h)] = sm
                 term = sm + m * (angle * rho)
                 total = term if total is None else total + term
-            kp[a, b, p, :, chunk(h)] = total
+            kp[b, a, p, :, chunk(h)] = total
 
     interior = list(range(1, PR - 1))
     edges = sorted({0, PR - 1})
 
     if interior:
-        @pl.loop(0, A)
+        @pl.loop(0, A, unroll=True)
         def _(a):
             for b in range(B):
                 for p in interior:
@@ -349,22 +359,24 @@
     def _():
         halo_down().wait_recv()
 
-    @pl.loop(0, A)
+    @pl.loop(0, A, unroll=True)
     def _(a):
         for b in range(B):
             for p in edges:
                 forward(a, b, p)
-        for g in range(G):
-            acc = None
-            for t in range(group):
-                y = split_dot(kp[a, g * group + t].reshape(PR * R, W), mat_ref[t])
-                acc = y if acc is None else acc + y
-            tmp[g, 0 : PR * R] = acc
-            even = tmp[g, pl.ds(0, PR * H, stride=2), :]
-            odd = tmp[g, pl.ds(1, PR * H, stride=2), :]
-            pooled[me, a, g] = ((even + odd) * (1.0 / (32.0 * math.pi))).reshape(PR, H, 128)
-        for d in range(1, n):
-            pool_copy(d, a).start()
+
+    for g in range(G):
+        acc = None
+        for t in range(group):
+            y = split_dot(kp[g * group + t].reshape(A * PR * R, W), mat_ref[t])
+            acc = y if acc is None else acc + y
+        tmp[g, 0 : A * PR * R] = acc
+    for g in range(G):
+        even = tmp[g, pl.ds(0, A * PR * H, stride=2), :]
+        odd = tmp[g, pl.ds(1, A * PR * H, stride=2), :]
+        pooled[me, g] = ((even + odd) * (1.0 / (32.0 * math.pi))).reshape(A, PR, H, 128)
+    for d in range(1, n):
+        row_copy(pooled, pool_send, pool_recv, d).start()
 
     @pl.when(has_high)
     def _():
@@ -380,19 +392,23 @@
     masks2 = lane_masks((H, 128), H, 1)
     racc[...] = jnp.zeros((NH * B + G, R, 128), f32)
 
-    @pl.loop(0, A)
-    def _(a):
-        for d in range(1, n):
-            pool_arrival(d, a).wait_recv()
-        left2 = [None] * H
-        for g in range(G):
-            f = [None] + [[pooled[i // PR, a, g, i % PR]] for i in range(H)] + [None]
-            source = conv_rows(f, H, masks2)
+    for d in range(1, n):
+        row_arrival(pooled, pool_send, pool_recv, d).wait_recv()
+
+    scale = 1.0 / (9.0 * 2.0 * math.pi * 16.0) / (18.0 * math.pi)
+    zero = jnp.zeros((H, 128), f32)
+    for g in range(G):
+        sources = []
+        for a in range(A):
+            f = [None] + [[pooled[i // PR, g, a, i % PR]] for i in range(H)] + [None]
+            sources.append(conv_rows(f, H, masks2))
+        cts = []
+        right2 = None
+        for a in range(A):
             ct = [None]
-            right2 = None
             for i in range(H):
                 m = gl2_ref[a, i] * gr2_ref[g : g + 1, :]
-                rho = source[i][0] * (il2_ref[a, i] * ir2_ref[g : g + 1, :])
+                rho = sources[a][i][0] * (il2_ref[a, i] * ir2_ref[g : g + 1, :])
                 sine, angle = arc_parts(rho)
                 pieces = []
                 for t in range(group):
@@ -402,31 +418,37 @@
                 ct.append([c * angle])
                 w = c * (m * sine)
                 right2 = w if right2 is None else right2 + w
-                left2[i] = w if left2[i] is None else left2[i] + w
+                wsum2[a, i] = w if g == 0 else wsum2[a, i] + w
             ct.append(None)
-            racc[NH * B + g, 0:H] = racc[NH * B + g, 0:H] + right2
-            b_rows = conv_rows(ct, H, masks2)
-            scale = 1.0 / (9.0 * 2.0 * math.pi * 16.0) / (18.0 * math.pi)
-            zero = jnp.zeros((H, 128), f32)
-            back[g, 0] = zero
-            back[g, H + 1] = zero
+            cts.append(ct)
+        racc[NH * B + g, 0:H] = right2
+        for a in range(A):
+            b_rows = conv_rows(cts[a], H, masks2)
+            back[a, 0] = zero
+            back[a, H + 1] = zero
             for i in range(H):
-                back[g, i + 1] = b_rows[i][0] * scale
-            x = back[g, pl.ds(me * PR, PR + 2)].reshape((PR + 2) * H, 128)
-            for t in range(group):
-                y = split_dot(x, mat_ref[t], ((1,), (1,)))
-                for h in range(NH):
-                    fine[a, g * group + t, h, pl.ds(0, (PR + 2) * H, stride=2), :] = y[:, chunk(h)]
-                    fine[a, g * group + t, h, pl.ds(1, (PR + 2) * H, stride=2), :] = y[:, chunk(h)]
-        for i in range(H):
-            wsum2[a, i] = left2[i]
-
+                back[a, i + 1] = b_rows[i][0] * scale
+        x = back[:, pl.ds(me * PR, PR + 2)].reshape(A * (PR + 2) * H, 128)
+        for t in range(group):
+            y = split_dot(x, mat_ref[t], ((1,), (1,)))
+            for h in range(NH):
+                fine[g * group + t, h, pl.ds(0, A * (PR + 2) * H, stride=2), :] = y[:, chunk(h)]
+                fine[g * group + t, h, pl.ds(1, A * (PR + 2) * H, stride=2), :] = y[:, chunk(h)]
+
+    def fine_row(a, b, h, c):
+        first = (a * (PR + 2) + c) * R
+        if not isinstance(first, int):
+            first = pl.multiple_of(first, 8)
+        return fine[b, h, pl.ds(first, R), :]
+
+    @pl.loop(0, A, unroll=True)
+    def _(a):
         lsum = [None] * rows
         for b in range(B):
             for h in range(NH):
                 total = None
                 for p in range(PR):
-                    bk = fine[a, b, h, (p + 1) * R : (p + 2) * R, :]
+                    bk = fine_row(a, b, h, p + 1)
                     for t in range(2):
                         i = 2 * p + t
                         w = bk * sinem[a, b, i, :, chunk(h)]
@@ -453,7 +475,7 @@
             if i not in cache:
                 c = (i + 1) // 2
                 cache[i] = [
-                    fine[a, b, h, c * R : (c + 1) * R, :] * slope[a, b, i, :, chunk(h)] for h in range(NH)
+                    fine_row(a, b, h, c) * slope[a, b, i, :, chunk(h)] for h in range(NH)
                 ]
             return cache[i]
 
@@ -462,19 +484,11 @@
             for h in range(NH):
                 out_v[a, b, i - 1, :, chunk(h)] = value[h]
 
-    def inner_out(a):
-        inner = pl.ds(1, rows - 2)
-        return pltpu.make_async_copy(out_v.at[a, :, inner], out_hbm.at[a, :, inner], out_sem.at[0, a])
-
-    def edge_out(a, i, s):
-        return pltpu.make_async_copy(out_v.at[a, :, i], out_hbm.at[a, :, i], out_sem.at[s, a])
-
     if rows > 2:
-        @pl.loop(0, A)
+        @pl.loop(0, A, unroll=True)
         def _(a):
             for b in range(B):
                 final(a, b, range(2, rows))
-            inner_out(a).start()
 
     for d in range(1, n):
         row_arrival(packet, left_send, left_recv, d).wait_recv()
@@ -508,12 +522,10 @@
     def _():
         slope_down().wait_recv()
 
-    @pl.loop(0, A)
+    @pl.loop(0, A, unroll=True)
     def _(a):
         for b in range(B):
             final(a, b, sorted({1, rows}))
-        edge_out(a, 0, 1).start()
-        edge_out(a, rows - 1, 2).start()
 
     inverse2 = il2_ref[...].reshape(A * H, H, 128)
     sums2 = split_dot(wsum2[...].reshape(A * H * H, 128), ones).reshape(A * H, H, 128)
@@ -542,23 +554,19 @@
     coarse = tmp[0, NH * B : NH * B + Gp, :]
     (coarse,) = conv_flat([coarse * (ir2_ref[...] * ir2_ref[...] * (1.0 / (4.0 * math.pi * 8.0)))], H, flat_masks2)
     wide = [split_dot(coarse, mat_ref[t], ((1,), (1,)), terms=3) for t in range(group)]
+    right_flat[...] = jnp.zeros((Bp, W), f32)
     for b in range(B):
-        right_out[b : b + 1, :] = wide[b % group][b // group : b // group + 1, :]
-    if Bp > B:
-        right_out[B:Bp, :] = jnp.zeros((Bp - B, W), f32)
+        right_flat[b : b + 1, :] = wide[b % group][b // group : b // group + 1, :]
     pieces = []
     for h in range(NH):
         scale = ir_ref[:, chunk(h)]
-        pieces.append(right_out[:, chunk(h)] + tmp[0, h * B : h * B + Bp, :] * (scale * scale * 4.5))
+        pieces.append(right_flat[:, chunk(h)] + tmp[0, h * B : h * B + Bp, :] * (scale * scale * 4.5))
     pieces = conv_flat(pieces, R, flat_masks)
     for h in range(NH):
-        right_out[:, chunk(h)] = pieces[h]
-
-    for a in range(A):
-        if rows > 2:
-            inner_out(a).wait()
-        edge_out(a, 0, 1).wait()
-        edge_out(a, rows - 1, 2).wait()
+        right_flat[:, chunk(h)] = pieces[h]
+    for b in range(B):
+        line = jnp.where(here, jnp.broadcast_to(right_flat[b : b + 1, :], (R, W)), 0.0)
+        right_out[b] = split_dot(line, choose, terms=3)[:, 0:R]
 
     @pl.when(has_high)
     def _():
@@ -573,10 +581,20 @@
     for d in range(1, n):
         row_copy(cot, cot_send, cot_recv, d).wait_send()
         row_copy(packet, left_send, left_recv, d).wait_send()
-        for a in range(A):
-            pool_copy(d, a).wait_send()
+        row_copy(pooled, pool_send, pool_recv, d).wait_send()
     for d in range(1, npair):
         pair_copy(d).wait_send()
+
+
+def store_body(a_ref, b_ref, c_ref, a_out, b_out, c_out, sems):
+    copies = [
+        pltpu.make_async_copy(source, target, sems.at[i])
+        for i, (source, target) in enumerate(((a_ref, a_out), (b_ref, b_out), (c_ref, c_out)))
+    ]
+    for c in copies:
+        c.start()
+    for c in copies:
+        c.wait()
 
 
 def on_device(n, npair, gram_field, left_variance, right_variance, cotangent):
@@ -590,41 +608,38 @@
     PR = rows // 2
     Bp, Gp = rounded(B), rounded(G)
     f32 = jnp.float32
-    right_flat = jnp.pad(right_variance.reshape(B, W), ((0, Bp - B), (0, 0)), constant_values=1.0)
 
     pair_rows = rounded(NH * B + G)
     packet_rows = rounded(A * rows + NH * B)
     sizes = (n, npair, A, B, rows, R, group, part)
     vmem = pl.BlockSpec(memory_space=pltpu.VMEM)
-    hbm = pl.BlockSpec(memory_space=pl.ANY)
+    hbm = pl.BlockSpec(memory_space=pltpu.HBM)
     dma = pltpu.SemaphoreType.DMA
 
     def scratch(*shape):
         return pltpu.VMEM(shape, f32)
 
-    out, left, right = pl.pallas_call(
+    shapes = tuple(
+        jax.ShapeDtypeStruct(x.shape, f32) for x in (gram_field, left_variance, right_variance)
+    )
+    results = pl.pallas_call(
         functools.partial(body, sizes),
-        out_shape=(
-            jax.ShapeDtypeStruct(gram_field.shape, f32),
-            jax.ShapeDtypeStruct((A, R, R), f32),
-            jax.ShapeDtypeStruct((Bp, W), f32),
-        ),
-        in_specs=[hbm, hbm, vmem, vmem],
-        out_specs=(hbm, vmem, vmem),
+        out_shape=shapes,
+        in_specs=[hbm] * 4,
+        out_specs=(vmem,) * 3,
         scratch_shapes=[
             scratch(A, B, rows + 2, R, W),
             scratch(n, A, part, H, H, width),
             scratch(A, B, rows + 2, R, W),
             scratch(A, B, rows, R, W),
-            scratch(A, B, PR, R, W),
-            scratch(G, max(PR * R, pair_rows + Gp, NH * B + Bp), 128),
-            scratch(n, A, G, PR, H, 128),
-            scratch(G, H + 2, H, 128),
-            scratch(A, B, NH, (PR + 2) * R, 128),
+            scratch(B, A, PR, R, W),
+            scratch(G, max(A * PR * R, pair_rows + Gp, NH * B + Bp), 128),
+            scratch(n, G, A, PR, H, 128),
+            scratch(A, H + 2, H, 128),
+            scratch(B, NH, A * (PR + 2) * R, 128),
             scratch(A, rows, R, 128),
             scratch(A, H, H, 128),
             scratch(NH * B + G, R, 128),
-            scratch(A, B, rows, R, W),
             scratch(n, packet_rows, 128),
             scratch(npair, pair_rows, 128),
             scratch(pair_rows, 128),
@@ -641,16 +656,26 @@
             scratch(A, R, R, 128),
             scratch(A, H * R, 128),
             scratch(R * R, 128),
-            dma((A + 1,)), dma((3, A)), dma((2,)), dma((2,)),
-            dma((n,)), dma((n,)), dma((n, A)), dma((n, A)),
+            scratch(A, R, R),
+            scratch(B, R, R),
+            scratch(Bp, W),
+            dma((A + 3,)), dma((2,)), dma((2,)),
+            dma((n,)), dma((n,)), dma((n,)), dma((n,)),
             dma((2,)), dma((2,)), dma((n,)), dma((n,)), dma((npair,)), dma((npair,)),
         ],
         compiler_params=pltpu.CompilerParams(
             collective_id=0, has_side_effects=True, vmem_limit_bytes=48 * 1024 * 1024
         ),
         name="arc_reverse",
-    )(gram_field, cotangent, left_variance, right_flat)
-    return out, left, right[:B].reshape(B, R, R)
+    )(gram_field, cotangent, left_variance, right_variance)
+    return pl.pallas_call(
+        store_body,
+        out_shape=shapes,
+        in_specs=[vmem] * 3,
+        out_specs=(hbm,) * 3,
+        scratch_shapes=[dma((3,))],
+        name="store_results",
+    )(*results)
 
 
 def solution(mesh):

time: 31.1 us -> 35.1 us (1.13)
  Pallas kernels: 24.2 us -> 28.4 us
    pallas_call x1 -> x2, Pallas kernels: 24.2 us -> 28.4 us  [the longest x1 26.1 us: on_device(): pl.pallas_call(functools.partial(body, sizes), out_shape=shapes, in_specs...]
    reshape x2 -> x0, local copies, waits for them, and re-layouts: 1.49 us -> none  [the longest x1 0.8 us: on_device(): right_variance.reshape(B, W)]
    unnamed x8 -> x14, local copies, waits for them, and re-layouts: 4.46 us -> 5.75 us
where the time goes in v3:
time: 35.1 us; the launch traced here: 34.8 us
  Pallas kernels  28.4 us (81%)
  local copies, waits for them, and re-layouts  5.75 us (16%)
  between operations  0.66 us (2%)
    pallas_call x1, Pallas kernels, on_device(): pl.pallas_call(functools.partial(body, sizes), out_shape=shapes, in_specs...  26.1 us
    unnamed x14, local copies, waits for them, and re-layouts  5.75 us
    pallas_call x1, Pallas kernels, on_device(): pl.pallas_call(store_body, out_shape=shapes, in_specs=[vmem] * 3, out_spe...  2.24 us

profile of v3, /device:TPU:0, one launch (start us, length us, event | category | flops | bytes accessed | tf_op | source)
XLA Modules:
  0.0 34.8 jit_solution(2685463360079410785)
XLA Ops:
  0.6 0.0 copy-start
  0.6 1.2 %copy-done = f32[4,2,8,16,256]{4,3,2,1,0:T(8,128)S(1)} copy-done((f32[4,2,8,16,256]{4,3,2,1,0:T(8,128)S(1)}, f32[4,2,8,16,256]{4,3,2,1,0:T(8,128)}, u32[]{:S(2)}) %copy-start) | copy-done | bytes 1048600
  1.9 0.0 copy-start.2
  1.9 0.9 %copy-done.2 = f32[4,1,8,8,64]{4,3,2,1,0:T(8,128)S(1)} copy-done((f32[4,1,8,8,64]{4,3,2,1,0:T(8,128)S(1)}, f32[4,1,8,8,64]{4,3,2,1,0:T(8,128)}, u32[]{:S(2)}) %copy-start.2) | copy-done | bytes 65560
  2.8 0.0 copy-start.3
  2.8 0.8 %copy-done.3 = f32[4,16,16]{2,1,0:T(8,128)S(1)} copy-done((f32[4,16,16]{2,1,0:T(8,128)S(1)}, f32[4,16,16]{2,1,0:T(8,128)}, u32[]{:S(2)}) %copy-start.3) | copy-done | bytes 4120
  3.5 0.0 copy-start.5
  3.5 0.7 %copy-done.5 = f32[2,16,16]{2,1,0:T(8,128)S(1)} copy-done((f32[2,16,16]{2,1,0:T(8,128)S(1)}, f32[2,16,16]{2,1,0:T(8,128)}, u32[]{:S(2)}) %copy-start.5) | copy-done | bytes 2072
  4.2 26.1 %arc_reverse.1 = (f32[4,2,8,16,256]{4,3,2,1,0:T(8,128)S(1)}, f32[4,16,16]{2,1,0:T(8,128)S(1)}, f32[2,16,16]{2,1,0:T(8,128)S(1)}) custom-call(f32[4,2,8,16,256]{4,3,2,1,0:T(8,128)S(1)} %copy-done, f32[4,1,8,8,64]{4,3,2,1,0:T(8,128)S(1)} %copy-done.2, f32[4,16,16]{2,1,0:T(8,128)S(1)} %copy-done.3, f32[2,16,16]{2,1,0:T(8,128)S(1)} %copy-done.5), custom_call_target="tpu_custom_call" | custom-call | tf_op jit(solution)/shard_map/arc_reverse/pallas_call | solution.py:625
  30.4 0.0 copy-start.1
  30.4 1.0 %copy-done.1 = f32[4,2,8,16,256]{4,3,2,1,0:T(8,128)} copy-done((f32[4,2,8,16,256]{4,3,2,1,0:T(8,128)}, f32[4,2,8,16,256]{4,3,2,1,0:T(8,128)S(1)}, u32[]{:S(2)}) %copy-start.1) | copy-done | bytes 1048600
  31.4 0.0 copy-start.4
  31.4 0.6 %copy-done.4 = f32[4,16,16]{2,1,0:T(8,128)} copy-done((f32[4,16,16]{2,1,0:T(8,128)}, f32[4,16,16]{2,1,0:T(8,128)S(1)}, u32[]{:S(2)}) %copy-start.4) | copy-done | bytes 4120
  32.0 0.0 copy-start.6
  32.0 0.6 %copy-done.6 = f32[2,16,16]{2,1,0:T(8,128)} copy-done((f32[2,16,16]{2,1,0:T(8,128)}, f32[2,16,16]{2,1,0:T(8,128)S(1)}, u32[]{:S(2)}) %copy-start.6) | copy-done | bytes 2072
  32.6 2.2 %store_results.1 = (f32[4,2,8,16,256]{4,3,2,1,0:T(8,128)}, f32[4,16,16]{2,1,0:T(8,128)}, f32[2,16,16]{2,1,0:T(8,128)}) custom-call(f32[4,2,8,16,256]{4,3,2,1,0:T(8,128)} %copy-done.1, f32[4,16,16]{2,1,0:T(8,128)} %copy-done.4, f32[2,16,16]{2,1,0:T(8,128)} %copy-done.6), custom_call_target="tpu_custom_call" | custom-call | tf_op jit(solution)/shard_map/store_results/pallas_call | solution.py:671
Async XLA Ops:
  0.6 1.2 %copy-start = (f32[4,2,8,16,256]{4,3,2,1,0:T(8,128)S(1)}, f32[4,2,8,16,256]{4,3,2,1,0:T(8,128)}, u32[]{:S(2)}) copy-start(f32[4,2,8,16,256]{4,3,2,1,0:T(8,128)} %gram_hbm.1) | copy-start | bytes 3145732
  1.9 0.9 %copy-start.2 = (f32[4,1,8,8,64]{4,3,2,1,0:T(8,128)S(1)}, f32[4,1,8,8,64]{4,3,2,1,0:T(8,128)}, u32[]{:S(2)}) copy-start(f32[4,1,8,8,64]{4,3,2,1,0:T(8,128)} %cot_hbm.1) | copy-start | bytes 196612
  2.8 0.8 %copy-start.3 = (f32[4,16,16]{2,1,0:T(8,128)S(1)}, f32[4,16,16]{2,1,0:T(8,128)}, u32[]{:S(2)}) copy-start(f32[4,16,16]{2,1,0:T(8,128)} %lv_hbm.1) | copy-start | bytes 12292
  3.5 0.7 %copy-start.5 = (f32[2,16,16]{2,1,0:T(8,128)S(1)}, f32[2,16,16]{2,1,0:T(8,128)}, u32[]{:S(2)}) copy-start(f32[2,16,16]{2,1,0:T(8,128)} %rv_hbm.1) | copy-start | bytes 6148
  30.4 1.0 %copy-start.1 = (f32[4,2,8,16,256]{4,3,2,1,0:T(8,128)}, f32[4,2,8,16,256]{4,3,2,1,0:T(8,128)S(1)}, u32[]{:S(2)}) copy-start(f32[4,2,8,16,256]{4,3,2,1,0:T(8,128)S(1)} %get-tuple-element.6.a_ref) | copy-start | bytes 3145732
  31.4 0.6 %copy-start.4 = (f32[4,16,16]{2,1,0:T(8,128)}, f32[4,16,16]{2,1,0:T(8,128)S(1)}, u32[]{:S(2)}) copy-start(f32[4,16,16]{2,1,0:T(8,128)S(1)} %get-tuple-element.7.b_ref) | copy-start | bytes 12292
  32.0 0.6 %copy-start.6 = (f32[2,16,16]{2,1,0:T(8,128)}, f32[2,16,16]{2,1,0:T(8,128)S(1)}, u32[]{:S(2)}) copy-start(f32[2,16,16]{2,1,0:T(8,128)S(1)} %get-tuple-element.8.c_ref) | copy-start | bytes 6148

commit v4 on v3

--- a/solution.py
+++ b/solution.py
@@ -152,11 +152,11 @@
 def body(
     sizes,
     gram_hbm, cot_hbm, lv_hbm, rv_hbm,
-    out_v, left_out, right_out,
-    gram, cot, slope, sinem, kp, tmp, pooled, back, fine, wsum, wsum2, racc, packet, pair_all, pair_packet,
+    out_hbm, left_out, right_out,
+    gram, cot, slope, sinem, kp, tmp, pooled, back, fine, wsum, wsum2, racc, out_v, packet, pair_all, pair_packet,
     gl_ref, il_ref, gl2_ref, il2_ref, gr_ref, ir_ref, gr2_ref, ir2_ref, mat_ref, lmap, cols, half_cols, ccol,
     lv_ref, rv_ref, right_flat,
-    load_sem, halo_send, halo_recv, cot_send, cot_recv, pool_send, pool_recv,
+    load_sem, out_sem, halo_send, halo_recv, cot_send, cot_recv, pool_send, pool_recv,
     slope_send, slope_recv, left_send, left_recv, pair_send, pair_recv,
 ):
     n, npair, A, B, rows, R, group, part = sizes
@@ -178,7 +178,9 @@
     barrier = pltpu.get_barrier_semaphore()
     for d in range(1, n):
         pl.semaphore_signal(barrier, inc=1, device_id={"row": lax.rem(me + d, n)})
-    for d in range(1, npair):
+
+    @pl.loop(1, npair)
+    def _(d):
         pl.semaphore_signal(barrier, inc=1, device_id={"pair": lax.rem(mine + d, npair)})
 
     loads = []
@@ -265,28 +267,26 @@
     sub16 = sub_of((R, 128))
     lane16 = lane_of((R, 128))
     band = jnp.abs(sub16 - lane16) <= 1
-    for a in range(A):
+
+    @pl.loop(0, A)
+    def _(a):
         v = lmap[a]
         v = v + jnp.where(sub16 + 1 < R, roll(v, -1, 0), 0.0) + jnp.where(sub16 >= 1, roll(v, 1, 0), 0.0)
-        lmap[a] = v
-    for a in range(A):
+        lines = []
         for i in range(R):
-            line = jnp.broadcast_to(lmap[a, i : i + 1, :], (R, 128))
-            cols[a, i] = jnp.where(band, line, 0.0)
-    spread = split_dot(cols[...].reshape(A * R * R, 128), ones, terms=3) * (1.0 / 9.0)
-    cols[...] = spread.reshape(A, R, R, 128)
-    for a in range(A):
+            lines.append(jnp.where(band, jnp.broadcast_to(v[i : i + 1, :], (R, 128)), 0.0))
+        spread = split_dot(jnp.concatenate(lines, axis=0), ones, terms=3) * (1.0 / 9.0)
+        cols[...] = spread.reshape(R, R, 128)
         for c in range(H):
-            half_cols[a, c * R : (c + 1) * R] = cols[a, 2 * c] + cols[a, 2 * c + 1]
-    for a in range(A):
-        even = half_cols[a, pl.ds(0, H * H, stride=2), :]
-        odd = half_cols[a, pl.ds(1, H * H, stride=2), :]
+            half_cols[c * R : (c + 1) * R] = cols[2 * c] + cols[2 * c + 1]
+        even = half_cols[pl.ds(0, H * H, stride=2), :]
+        odd = half_cols[pl.ds(1, H * H, stride=2), :]
         second = conv_columns(((even + odd) * 0.125).reshape(H, H, 128))
         for i in range(H):
             g2, i2 = root_pair(second[i])
             gl2_ref[a, i] = g2
             il2_ref[a, i] = i2 * (1.0 / 9.0)
-        g1, i1 = root_pair(cols[a, pl.ds(me * rows, rows)])
+        g1, i1 = root_pair(cols[pl.ds(me * rows, rows)])
         gl_ref[a] = g1
         il_ref[a] = i1 * (1.0 / 9.0)
 
@@ -341,29 +341,28 @@
                 total = term if total is None else total + term
             kp[b, a, p, :, chunk(h)] = total
 
-    interior = list(range(1, PR - 1))
-    edges = sorted({0, PR - 1})
-
-    if interior:
-        @pl.loop(0, A, unroll=True)
-        def _(a):
-            for b in range(B):
-                for p in interior:
-                    forward(a, b, p)
-
-    @pl.when(has_low)
-    def _():
-        halo_up().wait_recv()
-
-    @pl.when(has_high)
-    def _():
-        halo_down().wait_recv()
-
-    @pl.loop(0, A, unroll=True)
-    def _(a):
+    early = max(PR - 2, 0)
+
+    def ordered(step):
+        q = divided(step, A)
+        p = jnp.where(q < early, q + 1, jnp.where(q == PR - 2, 0, PR - 1))
+        return left_over(step, A), p
+
+    @pl.loop(0, A * PR)
+    def _(step):
+        @pl.when(step == early * A)
+        def _():
+            @pl.when(has_low)
+            def _():
+                halo_up().wait_recv()
+
+            @pl.when(has_high)
+            def _():
+                halo_down().wait_recv()
+
+        a, p = ordered(step)
         for b in range(B):
-            for p in edges:
-                forward(a, b, p)
+            forward(a, b, p)
 
     for g in range(G):
         acc = None
@@ -441,7 +440,7 @@
             first = pl.multiple_of(first, 8)
         return fine[b, h, pl.ds(first, R), :]
 
-    @pl.loop(0, A, unroll=True)
+    @pl.loop(0, A)
     def _(a):
         lsum = [None] * rows
         for b in range(B):
@@ -468,37 +467,19 @@
     for d in range(1, n):
         row_copy(packet, left_send, left_recv, d).start()
 
-    def final(a, b, chosen):
-        cache = {}
-
-        def product(i):
-            if i not in cache:
-                c = (i + 1) // 2
-                cache[i] = [
-                    fine_row(a, b, h, c) * slope[a, b, i, :, chunk(h)] for h in range(NH)
-                ]
-            return cache[i]
-
-        for i in chosen:
-            (value,) = conv_rows([product(i - 1), product(i), product(i + 1)], R, masks)
+    def final(a, b, p):
+        f = [
+            [fine_row(a, b, h, p + (t + 1) // 2) * slope[a, b, 2 * p + t, :, chunk(h)] for h in range(NH)]
+            for t in range(4)
+        ]
+        value = conv_rows(f, R, masks)
+        for t in range(2):
             for h in range(NH):
-                out_v[a, b, i - 1, :, chunk(h)] = value[h]
-
-    if rows > 2:
-        @pl.loop(0, A, unroll=True)
-        def _(a):
-            for b in range(B):
-                final(a, b, range(2, rows))
-
-    for d in range(1, n):
-        row_arrival(packet, left_send, left_recv, d).wait_recv()
-    right = packet[0, LR : LR + NH * B, :]
-    for r in range(1, n):
-        right = right + packet[r, LR : LR + NH * B, :]
-    pair_packet[...] = jnp.zeros(pair_packet.shape, f32)
-    pair_packet[0 : NH * B, :] = right
-    pair_packet[NH * B : NH * B + G, :] = right_sums[NH * B : NH * B + G]
-    pair_all[mine] = pair_packet[...]
+                out_v[a, b, 2 * p + t, :, chunk(h)] = value[t][h]
+
+    def store(a, p):
+        two = pl.ds(2 * p, 2)
+        return pltpu.make_async_copy(out_v.at[a, :, two], out_hbm.at[a, :, two], out_sem.at[a, p])
 
     def pair_copy(d):
         return pltpu.make_async_remote_copy(
@@ -511,39 +492,59 @@
             src_ref=pair_packet, dst_ref=pair_all.at[source], send_sem=pair_send.at[d],
             recv_sem=pair_recv.at[source], device_id={"pair": source})
 
-    for d in range(1, npair):
-        pair_copy(d).start()
-
-    @pl.when(has_low)
-    def _():
-        slope_up().wait_recv()
-
-    @pl.when(has_high)
-    def _():
-        slope_down().wait_recv()
-
-    @pl.loop(0, A, unroll=True)
-    def _(a):
+    pair_packet[...] = jnp.zeros(pair_packet.shape, f32)
+    pair_packet[NH * B : NH * B + G, :] = right_sums[NH * B : NH * B + G]
+
+    @pl.loop(0, A * PR)
+    def _(step):
+        @pl.when(step == early * A)
+        def _():
+            for d in range(1, n):
+                row_arrival(packet, left_send, left_recv, d).wait_recv()
+            right = packet[0, LR : LR + NH * B, :]
+            for r in range(1, n):
+                right = right + packet[r, LR : LR + NH * B, :]
+            pair_packet[0 : NH * B, :] = right
+            pair_all[mine] = pair_packet[...]
+
+            @pl.loop(1, npair)
+            def _(d):
+                pair_copy(d).start()
+
+            @pl.when(has_low)
+            def _():
+                slope_up().wait_recv()
+
+            @pl.when(has_high)
+            def _():
+                slope_down().wait_recv()
+
+        a, p = ordered(step)
         for b in range(B):
-            final(a, b, sorted({1, rows}))
+            final(a, b, p)
+        store(a, p).start()
 
     inverse2 = il2_ref[...].reshape(A * H, H, 128)
     sums2 = split_dot(wsum2[...].reshape(A * H * H, 128), ones).reshape(A * H, H, 128)
     sums2 = sums2 * (inverse2 * inverse2 * (81.0 / (4.0 * math.pi * 8.0)))
-    for a in range(A):
-        mixed = conv_columns(sums2[a * H : (a + 1) * H])
+    wsum2[...] = sums2.reshape(A, H, H, 128)
+
+    @pl.loop(0, A)
+    def _(a):
+        mixed = conv_columns(wsum2[a])
         for c in range(H):
             for t in range(2):
                 ccol[pl.ds((2 * c + t) * R, H, stride=2), :] = mixed[c]
                 ccol[pl.ds((2 * c + t) * R + 1, H, stride=2), :] = mixed[c]
         coarse = jnp.sum(jnp.where(diagonal, ccol[...].reshape(R, R, 128), 0.0), axis=1)
-        local = jnp.concatenate([packet[r, a * rows : (a + 1) * rows, :] for r in range(n)], axis=0)
+        local = jnp.concatenate([packet[r, pl.ds(a * rows, rows), :] for r in range(n)], axis=0)
         v = coarse + local
         v = v + jnp.where(sub16 + 1 < R, roll(v, -1, 0), 0.0) + jnp.where(sub16 >= 1, roll(v, 1, 0), 0.0)
         v = (v + roll(v, 1, 1) + roll(v, -1, 1)) * (1.0 / 9.0)
         left_out[a] = v[:, 0:R]
 
-    for d in range(1, npair):
+    @pl.loop(1, npair)
+    def _(d):
         pair_arrival(d).wait_recv()
     total = pair_all[0]
     for r in range(1, npair):
@@ -568,6 +569,11 @@
         line = jnp.where(here, jnp.broadcast_to(right_flat[b : b + 1, :], (R, W)), 0.0)
         right_out[b] = split_dot(line, choose, terms=3)[:, 0:R]
 
+    @pl.loop(0, A * PR)
+    def _(step):
+        a, p = ordered(step)
+        store(a, p).wait()
+
     @pl.when(has_high)
     def _():
         halo_up().wait_send()
@@ -582,19 +588,10 @@
         row_copy(cot, cot_send, cot_recv, d).wait_send()
         row_copy(packet, left_send, left_recv, d).wait_send()
         row_copy(pooled, pool_send, pool_recv, d).wait_send()
-    for d in range(1, npair):
+
+    @pl.loop(1, npair)
+    def _(d):
         pair_copy(d).wait_send()
-
-
-def store_body(a_ref, b_ref, c_ref, a_out, b_out, c_out, sems):
-    copies = [
-        pltpu.make_async_copy(source, target, sems.at[i])
-        for i, (source, target) in enumerate(((a_ref, a_out), (b_ref, b_out), (c_ref, c_out)))
-    ]
-    for c in copies:
-        c.start()
-    for c in copies:
-        c.wait()
 
 
 def on_device(n, npair, gram_field, left_variance, right_variance, cotangent):
@@ -613,7 +610,7 @@
     packet_rows = rounded(A * rows + NH * B)
     sizes = (n, npair, A, B, rows, R, group, part)
     vmem = pl.BlockSpec(memory_space=pltpu.VMEM)
-    hbm = pl.BlockSpec(memory_space=pltpu.HBM)
+    hbm = pl.BlockSpec(memory_space=pl.ANY)
     dma = pltpu.SemaphoreType.DMA
 
     def scratch(*shape):
@@ -622,11 +619,11 @@
     shapes = tuple(
         jax.ShapeDtypeStruct(x.shape, f32) for x in (gram_field, left_variance, right_variance)
     )
-    results = pl.pallas_call(
+    return pl.pallas_call(
         functools.partial(body, sizes),
         out_shape=shapes,
         in_specs=[hbm] * 4,
-        out_specs=(vmem,) * 3,
+        out_specs=(hbm, vmem, vmem),
         scratch_shapes=[
             scratch(A, B, rows + 2, R, W),
             scratch(n, A, part, H, H, width),
@@ -640,6 +637,7 @@
             scratch(A, rows, R, 128),
             scratch(A, H, H, 128),
             scratch(NH * B + G, R, 128),
+            scratch(A, B, rows, R, W),
             scratch(n, packet_rows, 128),
             scratch(npair, pair_rows, 128),
             scratch(pair_rows, 128),
@@ -653,29 +651,21 @@
             scratch(Gp, 128),
             pltpu.VMEM((group, W, 128), jnp.bfloat16),
             scratch(A, R, 128),
-            scratch(A, R, R, 128),
-            scratch(A, H * R, 128),
+            scratch(R, R, 128),
+            scratch(H * R, 128),
             scratch(R * R, 128),
             scratch(A, R, R),
             scratch(B, R, R),
             scratch(Bp, W),
-            dma((A + 3,)), dma((2,)), dma((2,)),
+            dma((A + 3,)), dma((A, PR)), dma((2,)), dma((2,)),
             dma((n,)), dma((n,)), dma((n,)), dma((n,)),
             dma((2,)), dma((2,)), dma((n,)), dma((n,)), dma((npair,)), dma((npair,)),
         ],
         compiler_params=pltpu.CompilerParams(
-            collective_id=0, has_side_effects=True, vmem_limit_bytes=48 * 1024 * 1024
+            collective_id=0, has_side_effects=True, vmem_limit_bytes=64 * 1024 * 1024
         ),
         name="arc_reverse",
     )(gram_field, cotangent, left_variance, right_variance)
-    return pl.pallas_call(
-        store_body,
-        out_shape=shapes,
-        in_specs=[vmem] * 3,
-        out_specs=(hbm,) * 3,
-        scratch_shapes=[dma((3,))],
-        name="store_results",
-    )(*results)
 
 
 def solution(mesh):

time: 35.1 us -> 31.2 us (0.89)
  local copies, waits for them, and re-layouts: 5.75 us -> 3.61 us
  Pallas kernels: 28.4 us -> 26.7 us
    pallas_call x1 -> x0, Pallas kernels: 2.24 us -> none  [on_device(): pl.pallas_call(store_body, out_shape=shapes, in_specs=[vmem] * 3, out_spe...]
    unnamed x14 -> x7, local copies, waits for them, and re-layouts: 5.75 us -> 3.61 us
    pallas_call x1, Pallas kernels: 26.1 us -> 26.7 us  [on_device(): pl.pallas_call(functools.partial(body, sizes), out_shape=shapes, in_specs...]
where the time goes in v4:
time: 31.2 us; the launch traced here: 31 us
  Pallas kernels  26.7 us (86%)
  local copies, waits for them, and re-layouts  3.61 us (12%)
  between operations  0.65 us (2%)
    pallas_call x1, Pallas kernels, on_device(): pl.pallas_call(functools.partial(body, sizes), out_shape=shapes, in_specs...  26.7 us
    unnamed x7, local copies, waits for them, and re-layouts  3.61 us

profile of v4, /device:TPU:0, one launch (start us, length us, event | category | flops | bytes accessed | tf_op | source)
XLA Modules:
  0.0 31.0 jit_solution(13728952043002024213)
XLA Ops:
  0.6 26.7 %arc_reverse.1 = (f32[4,2,8,16,256]{4,3,2,1,0:T(8,128)}, f32[4,16,16]{2,1,0:T(8,128)}, f32[2,16,16]{2,1,0:T(8,128)}) custom-call(f32[4,2,8,16,256]{4,3,2,1,0:T(8,128)} %gram_hbm.1, f32[4,1,8,8,64]{4,3,2,1,0:T(8,128)} %cot_hbm.1, f32[4,16,16]{2,1,0:T(8,128)} %lv_hbm.1, f32[2,16,16]{2,1,0:T(8,128)} %rv_hbm.1), custom_call_target="tpu_custom_call" | custom-call | tf_op jit(solution)/shard_map/arc_reverse/pallas_call | solution.py:622
  27.4 0.0 copy-start
  27.4 2.3 %copy.10 = f32[4,2,8,16,256]{4,3,2,1,0:T(8,128)} copy(f32[4,2,8,16,256]{4,3,2,1,0:T(8,128)} %get-tuple-element.6) | data formatting | bytes 2097152
  29.7 0.0 copy-done
  29.7 0.0 copy-start.1
  29.7 0.6 %copy.11 = f32[4,16,16]{2,1,0:T(8,128)} copy(f32[4,16,16]{2,1,0:T(8,128)S(1)} %copy-done) | data formatting | bytes 8192
  30.3 0.1 copy-done.1
  30.4 0.6 %copy.12 = f32[2,16,16]{2,1,0:T(8,128)} copy(f32[2,16,16]{2,1,0:T(8,128)S(1)} %copy-done.1) | data formatting | bytes 4096
Async XLA Ops:
  27.4 2.3 %copy-start = (f32[4,16,16]{2,1,0:T(8,128)S(1)}, f32[4,16,16]{2,1,0:T(8,128)}, u32[]{:S(2)}) copy-start(f32[4,16,16]{2,1,0:T(8,128)} %get-tuple-element.7) | copy-start | bytes 12292
  29.7 0.7 %copy-start.1 = (f32[2,16,16]{2,1,0:T(8,128)S(1)}, f32[2,16,16]{2,1,0:T(8,128)}, u32[]{:S(2)}) copy-start(f32[2,16,16]{2,1,0:T(8,128)} %get-tuple-element.8) | copy-start | bytes 6148

commit v5 on v4

--- a/solution.py
+++ b/solution.py
@@ -343,14 +343,17 @@
 
     early = max(PR - 2, 0)
 
+    block = 2 if A % 2 == 0 else 1
+    turns = A // block
+
     def ordered(step):
-        q = divided(step, A)
+        q = divided(step, turns)
         p = jnp.where(q < early, q + 1, jnp.where(q == PR - 2, 0, PR - 1))
-        return left_over(step, A), p
-
-    @pl.loop(0, A * PR)
+        return left_over(step, turns) * block, p
+
+    @pl.loop(0, turns * PR)
     def _(step):
-        @pl.when(step == early * A)
+        @pl.when(step == early * turns)
         def _():
             @pl.when(has_low)
             def _():
@@ -361,8 +364,9 @@
                 halo_down().wait_recv()
 
         a, p = ordered(step)
-        for b in range(B):
-            forward(a, b, p)
+        for t in range(block):
+            for b in range(B):
+                forward(a + t, b, p)
 
     for g in range(G):
         acc = None
@@ -394,7 +398,7 @@
     for d in range(1, n):
         row_arrival(pooled, pool_send, pool_recv, d).wait_recv()
 
-    scale = 1.0 / (9.0 * 2.0 * math.pi * 16.0) / (18.0 * math.pi)
+    scale = 2.0 / (9.0 * 2.0 * math.pi * 16.0) / (18.0 * math.pi)
     zero = jnp.zeros((H, 128), f32)
     for g in range(G):
         sources = []
@@ -460,7 +464,7 @@
     diagonal = (sub16 == lane16)[None]
     sums = split_dot(wsum[...].reshape(LR * R, 128), ones).reshape(LR, R, 128)
     inverse = il_ref[...].reshape(LR, R, 128)
-    sums = sums * (inverse * inverse * (4.5 * 81.0))
+    sums = sums * (inverse * inverse * (2.25 * 81.0))
     packet[me, 0:LR, :] = jnp.sum(jnp.where(diagonal, sums, 0.0), axis=1)
     right_sums = jnp.sum(racc[...], axis=1)
     packet[me, LR : LR + NH * B, :] = right_sums[0 : NH * B]
@@ -479,7 +483,8 @@
 
     def store(a, p):
         two = pl.ds(2 * p, 2)
-        return pltpu.make_async_copy(out_v.at[a, :, two], out_hbm.at[a, :, two], out_sem.at[a, p])
+        some = pl.ds(a, block)
+        return pltpu.make_async_copy(out_v.at[some, :, two], out_hbm.at[some, :, two], out_sem.at[a, p])
 
     def pair_copy(d):
         return pltpu.make_async_remote_copy(
@@ -495,9 +500,9 @@
     pair_packet[...] = jnp.zeros(pair_packet.shape, f32)
     pair_packet[NH * B : NH * B + G, :] = right_sums[NH * B : NH * B + G]
 
-    @pl.loop(0, A * PR)
+    @pl.loop(0, turns * PR)
     def _(step):
-        @pl.when(step == early * A)
+        @pl.when(step == early * turns)
         def _():
             for d in range(1, n):
                 row_arrival(packet, left_send, left_recv, d).wait_recv()
@@ -520,8 +525,9 @@
                 slope_down().wait_recv()
 
         a, p = ordered(step)
-        for b in range(B):
-            final(a, b, p)
+        for t in range(block):
+            for b in range(B):
+                final(a + t, b, p)
         store(a, p).start()
 
     inverse2 = il2_ref[...].reshape(A * H, H, 128)
@@ -561,7 +567,7 @@
     pieces = []
     for h in range(NH):
         scale = ir_ref[:, chunk(h)]
-        pieces.append(right_flat[:, chunk(h)] + tmp[0, h * B : h * B + Bp, :] * (scale * scale * 4.5))
+        pieces.append(right_flat[:, chunk(h)] + tmp[0, h * B : h * B + Bp, :] * (scale * scale * 2.25))
     pieces = conv_flat(pieces, R, flat_masks)
     for h in range(NH):
         right_flat[:, chunk(h)] = pieces[h]
@@ -569,7 +575,7 @@
         line = jnp.where(here, jnp.broadcast_to(right_flat[b : b + 1, :], (R, W)), 0.0)
         right_out[b] = split_dot(line, choose, terms=3)[:, 0:R]
 
-    @pl.loop(0, A * PR)
+    @pl.loop(0, turns * PR)
     def _(step):
         a, p = ordered(step)
         store(a, p).wait()
@@ -619,7 +625,7 @@
     shapes = tuple(
         jax.ShapeDtypeStruct(x.shape, f32) for x in (gram_field, left_variance, right_variance)
     )
-    return pl.pallas_call(
+    out, left, right = pl.pallas_call(
         functools.partial(body, sizes),
         out_shape=shapes,
         in_specs=[hbm] * 4,
@@ -666,6 +672,7 @@
         ),
         name="arc_reverse",
     )(gram_field, cotangent, left_variance, right_variance)
+    return out * 0.5, left, right
 
 
 def solution(mesh):

time: 31.2 us -> 30.7 us (0.984)
  other arithmetic: 0 us -> 2.34 us
  local copies, waits for them, and re-layouts: 3.61 us -> 1.34 us
  Pallas kernels: 26.7 us -> 26.1 us
    mul x0 -> x1, other arithmetic: none -> 2.34 us  [on_device(): return (out * 0.5, left, right)]
    unnamed x7 -> x6, local copies, waits for them, and re-layouts: 3.61 us -> 1.34 us
    pallas_call x1, Pallas kernels: 26.7 us -> 26.1 us  [on_device(): pl.pallas_call(functools.partial(body, sizes), out_shape=shapes, in_specs...]
where the time goes in v5:
time: 30.7 us; the launch traced here: 30.4 us
  Pallas kernels  26.1 us (85%)
  other arithmetic  2.34 us (8%)
  local copies, waits for them, and re-layouts  1.34 us (4%)
  between operations  0.65 us (2%)
    pallas_call x1, Pallas kernels, on_device(): pl.pallas_call(functools.partial(body, sizes), out_shape=shapes, in_specs...  26.1 us
    mul x1, other arithmetic, on_device(): return (out * 0.5, left, right)  2.34 us
    unnamed x6, local copies, waits for them, and re-layouts  1.34 us

profile of v5, /device:TPU:0, one launch (start us, length us, event | category | flops | bytes accessed | tf_op | source)
XLA Modules:
  0.0 30.4 jit_solution(6348085388029774025)
XLA Ops:
  0.6 26.1 %arc_reverse.1 = (f32[4,2,8,16,256]{4,3,2,1,0:T(8,128)}, f32[4,16,16]{2,1,0:T(8,128)}, f32[2,16,16]{2,1,0:T(8,128)}) custom-call(f32[4,2,8,16,256]{4,3,2,1,0:T(8,128)} %gram_hbm.1, f32[4,1,8,8,64]{4,3,2,1,0:T(8,128)} %cot_hbm.1, f32[4,16,16]{2,1,0:T(8,128)} %lv_hbm.1, f32[2,16,16]{2,1,0:T(8,128)} %rv_hbm.1), custom_call_target="tpu_custom_call" | custom-call | tf_op jit(solution)/shard_map/arc_reverse/pallas_call | solution.py:628
  26.7 0.0 copy-start
  26.8 2.3 %broadcast_multiply_fusion = f32[4,2,8,16,256]{4,3,2,1,0:T(8,128)} fusion(f32[4,2,8,16,256]{4,3,2,1,0:T(8,128)} %get-tuple-element.6), kind=kLoop, calls=%fused_computation | loop fusion | flops 262144 | bytes 2097152 | tf_op jit(solution)/shard_map/mul | solution.py:675
  29.1 0.0 copy-done
  29.1 0.0 copy-start.1
  29.1 0.6 %copy.9 = f32[4,16,16]{2,1,0:T(8,128)} copy(f32[4,16,16]{2,1,0:T(8,128)S(1)} %copy-done) | data formatting | bytes 8192
  29.7 0.1 copy-done.1
  29.8 0.6 %copy.10 = f32[2,16,16]{2,1,0:T(8,128)} copy(f32[2,16,16]{2,1,0:T(8,128)S(1)} %copy-done.1) | data formatting | bytes 4096
Async XLA Ops:
  26.7 2.4 %copy-start = (f32[4,16,16]{2,1,0:T(8,128)S(1)}, f32[4,16,16]{2,1,0:T(8,128)}, u32[]{:S(2)}) copy-start(f32[4,16,16]{2,1,0:T(8,128)} %get-tuple-element.13) | copy-start | bytes 12292
  29.1 0.7 %copy-start.1 = (f32[2,16,16]{2,1,0:T(8,128)S(1)}, f32[2,16,16]{2,1,0:T(8,128)}, u32[]{:S(2)}) copy-start(f32[2,16,16]{2,1,0:T(8,128)} %get-tuple-element.14) | copy-start | bytes 6148

commit v6 on v5

--- a/solution.py
+++ b/solution.py
@@ -151,12 +151,12 @@
 
 def body(
     sizes,
-    gram_hbm, cot_hbm, lv_hbm, rv_hbm,
-    out_hbm, left_out, right_out,
-    gram, cot, slope, sinem, kp, tmp, pooled, back, fine, wsum, wsum2, racc, out_v, packet, pair_all, pair_packet,
+    gram_hbm, cot_hbm, maps_hbm,
+    out_v, left_out, right_out,
+    gram, cot, slope, sinem, kp, tmp, pooled, back, fine, wsum, wsum2, racc, packet, pair_all, pair_packet,
     gl_ref, il_ref, gl2_ref, il2_ref, gr_ref, ir_ref, gr2_ref, ir2_ref, mat_ref, lmap, cols, half_cols, ccol,
     lv_ref, rv_ref, right_flat,
-    load_sem, out_sem, halo_send, halo_recv, cot_send, cot_recv, pool_send, pool_recv,
+    load_sem, halo_send, halo_recv, cot_send, cot_recv, pool_send, pool_recv,
     slope_send, slope_recv, left_send, left_recv, pair_send, pair_recv,
 ):
     n, npair, A, B, rows, R, group, part = sizes
@@ -190,9 +190,9 @@
         loads.append(c)
     cot_load = pltpu.make_async_copy(cot_hbm, cot.at[me], load_sem.at[A])
     cot_load.start()
-    left_load = pltpu.make_async_copy(lv_hbm, lv_ref, load_sem.at[A + 1])
+    left_load = pltpu.make_async_copy(maps_hbm.at[pl.ds(0, A)], lv_ref, load_sem.at[A + 1])
     left_load.start()
-    right_load = pltpu.make_async_copy(rv_hbm, rv_ref, load_sem.at[A + 2])
+    right_load = pltpu.make_async_copy(maps_hbm.at[pl.ds(A, B)], rv_ref, load_sem.at[A + 2])
     right_load.start()
 
     pl.semaphore_wait(barrier, n - 1 + npair - 1)
@@ -398,7 +398,7 @@
     for d in range(1, n):
         row_arrival(pooled, pool_send, pool_recv, d).wait_recv()
 
-    scale = 2.0 / (9.0 * 2.0 * math.pi * 16.0) / (18.0 * math.pi)
+    scale = 1.0 / (9.0 * 2.0 * math.pi * 16.0) / (18.0 * math.pi)
     zero = jnp.zeros((H, 128), f32)
     for g in range(G):
         sources = []
@@ -464,7 +464,7 @@
     diagonal = (sub16 == lane16)[None]
     sums = split_dot(wsum[...].reshape(LR * R, 128), ones).reshape(LR, R, 128)
     inverse = il_ref[...].reshape(LR, R, 128)
-    sums = sums * (inverse * inverse * (2.25 * 81.0))
+    sums = sums * (inverse * inverse * (4.5 * 81.0))
     packet[me, 0:LR, :] = jnp.sum(jnp.where(diagonal, sums, 0.0), axis=1)
     right_sums = jnp.sum(racc[...], axis=1)
     packet[me, LR : LR + NH * B, :] = right_sums[0 : NH * B]
@@ -480,11 +480,6 @@
         for t in range(2):
             for h in range(NH):
                 out_v[a, b, 2 * p + t, :, chunk(h)] = value[t][h]
-
-    def store(a, p):
-        two = pl.ds(2 * p, 2)
-        some = pl.ds(a, block)
-        return pltpu.make_async_copy(out_v.at[some, :, two], out_hbm.at[some, :, two], out_sem.at[a, p])
 
     def pair_copy(d):
         return pltpu.make_async_remote_copy(
@@ -528,7 +523,6 @@
         for t in range(block):
             for b in range(B):
                 final(a + t, b, p)
-        store(a, p).start()
 
     inverse2 = il2_ref[...].reshape(A * H, H, 128)
     sums2 = split_dot(wsum2[...].reshape(A * H * H, 128), ones).reshape(A * H, H, 128)
@@ -567,18 +561,13 @@
     pieces = []
     for h in range(NH):
         scale = ir_ref[:, chunk(h)]
-        pieces.append(right_flat[:, chunk(h)] + tmp[0, h * B : h * B + Bp, :] * (scale * scale * 2.25))
+        pieces.append(right_flat[:, chunk(h)] + tmp[0, h * B : h * B + Bp, :] * (scale * scale * 4.5))
     pieces = conv_flat(pieces, R, flat_masks)
     for h in range(NH):
         right_flat[:, chunk(h)] = pieces[h]
     for b in range(B):
         line = jnp.where(here, jnp.broadcast_to(right_flat[b : b + 1, :], (R, W)), 0.0)
         right_out[b] = split_dot(line, choose, terms=3)[:, 0:R]
-
-    @pl.loop(0, turns * PR)
-    def _(step):
-        a, p = ordered(step)
-        store(a, p).wait()
 
     @pl.when(has_high)
     def _():
@@ -625,11 +614,11 @@
     shapes = tuple(
         jax.ShapeDtypeStruct(x.shape, f32) for x in (gram_field, left_variance, right_variance)
     )
-    out, left, right = pl.pallas_call(
+    return pl.pallas_call(
         functools.partial(body, sizes),
         out_shape=shapes,
-        in_specs=[hbm] * 4,
-        out_specs=(hbm, vmem, vmem),
+        in_specs=[hbm] * 3,
+        out_specs=(vmem, vmem, vmem),
         scratch_shapes=[
             scratch(A, B, rows + 2, R, W),
             scratch(n, A, part, H, H, width),
@@ -643,7 +632,6 @@
             scratch(A, rows, R, 128),
             scratch(A, H, H, 128),
             scratch(NH * B + G, R, 128),
-            scratch(A, B, rows, R, W),
             scratch(n, packet_rows, 128),
             scratch(npair, pair_rows, 128),
             scratch(pair_rows, 128),
@@ -663,16 +651,15 @@
             scratch(A, R, R),
             scratch(B, R, R),
             scratch(Bp, W),
-            dma((A + 3,)), dma((A, PR)), dma((2,)), dma((2,)),
+            dma((A + 3,)), dma((2,)), dma((2,)),
             dma((n,)), dma((n,)), dma((n,)), dma((n,)),
             dma((2,)), dma((2,)), dma((n,)), dma((n,)), dma((npair,)), dma((npair,)),
         ],
         compiler_params=pltpu.CompilerParams(
-            collective_id=0, has_side_effects=True, vmem_limit_bytes=64 * 1024 * 1024
+            collective_id=0, has_side_effects=True, vmem_limit_bytes=int(52 * 2**20)
         ),
         name="arc_reverse",
-    )(gram_field, cotangent, left_variance, right_variance)
-    return out * 0.5, left, right
+    )(gram_field, cotangent, jnp.concatenate([left_variance, right_variance], axis=0))
 
 
 def solution(mesh):

time: 30.7 us -> 29.9 us (0.974)
  local copies, waits for them, and re-layouts: 1.34 us -> 3.09 us
  other arithmetic: 2.34 us -> 0.78 us
  Pallas kernels: 26.1 us -> 25.2 us
    mul x1 -> x0, other arithmetic: 2.34 us -> none  [on_device(): return (out * 0.5, left, right)]
    unnamed x6 -> x5, local copies, waits for them, and re-layouts: 1.34 us -> 3.09 us
    pallas_call x1, Pallas kernels: 26.1 us -> 25.2 us  [on_device(): pl.pallas_call(functools.partial(body, sizes), out_shape=shapes, in_specs...]
    concatenate x0 -> x1, other arithmetic: none -> 0.78 us  [on_device(): jnp.concatenate([left_variance, right_variance], axis=0)]
where the time goes in v6:
time: 29.9 us; the launch traced here: 29.7 us
  Pallas kernels  25.2 us (84%)
  local copies, waits for them, and re-layouts  3.09 us (10%)
  other arithmetic  0.78 us (3%)
  between operations  0.64 us (2%)
    pallas_call x1, Pallas kernels, on_device(): pl.pallas_call(functools.partial(body, sizes), out_shape=shapes, in_specs...  25.2 us
    unnamed x5, local copies, waits for them, and re-layouts  3.09 us
    concatenate x1, other arithmetic, on_device(): jnp.concatenate([left_variance, right_variance], axis=0)  0.78 us

profile of v6, /device:TPU:0, one launch (start us, length us, event | category | flops | bytes accessed | tf_op | source)
XLA Modules:
  0.0 29.7 jit_solution(10289104079193315612)
XLA Ops:
  0.6 0.8 %pad_maximum_fusion.maps_hbm = f32[6,16,16]{2,1,0:T(8,128)S(1)} fusion(f32[2,16,16]{2,1,0:T(8,128)} %param.6, f32[4,16,16]{2,1,0:T(8,128)} %param.5), kind=kLoop, calls=%fused_computation | loop fusion | flops 1536 | bytes 12288 | tf_op jit(solution)/shard_map/concatenate | solution.py:662
  1.4 0.0 copy-start
  1.4 0.9 %copy-done = f32[4,1,8,8,64]{4,3,2,1,0:T(8,128)S(1)} copy-done((f32[4,1,8,8,64]{4,3,2,1,0:T(8,128)S(1)}, f32[4,1,8,8,64]{4,3,2,1,0:T(8,128)}, u32[]{:S(2)}) %copy-start) | copy-done | bytes 65560
  2.3 25.2 %arc_reverse.1 = (f32[4,2,8,16,256]{4,3,2,1,0:T(8,128)S(1)}, f32[4,16,16]{2,1,0:T(8,128)S(1)}, f32[2,16,16]{2,1,0:T(8,128)S(1)}) custom-call(f32[4,2,8,16,256]{4,3,2,1,0:T(8,128)} %gram_hbm.1, f32[4,1,8,8,64]{4,3,2,1,0:T(8,128)S(1)} %copy-done, f32[6,16,16]{2,1,0:T(8,128)S(1)} %pad_maximum_fusion.maps_hbm), custom_call_target="tpu_custom_call" | custom-call | tf_op jit(solution)/shard_map/arc_reverse/pallas_call | solution.py:617
  27.5 1.0 %copy.10 = f32[4,2,8,16,256]{4,3,2,1,0:T(8,128)} copy(f32[4,2,8,16,256]{4,3,2,1,0:T(8,128)S(1)} %get-tuple-element.6) | data formatting | bytes 2097152
  28.5 0.6 %copy.11 = f32[4,16,16]{2,1,0:T(8,128)} copy(f32[4,16,16]{2,1,0:T(8,128)S(1)} %get-tuple-element.7) | data formatting | bytes 8192
  29.1 0.6 %copy.12 = f32[2,16,16]{2,1,0:T(8,128)} copy(f32[2,16,16]{2,1,0:T(8,128)S(1)} %get-tuple-element.8) | data formatting | bytes 4096
Async XLA Ops:
  1.4 0.9 %copy-start = (f32[4,1,8,8,64]{4,3,2,1,0:T(8,128)S(1)}, f32[4,1,8,8,64]{4,3,2,1,0:T(8,128)}, u32[]{:S(2)}) copy-start(f32[4,1,8,8,64]{4,3,2,1,0:T(8,128)} %cot_hbm.1) | copy-start | bytes 196612
